TPU v7x, 32 devices: a whole 2x2x4 slice. The times are simulated.
32 devices in a mesh: rows: 8 (over z, x), tp: 4 (over y, core).
Axes of the slice: x: 2, y: 2, z: 4, core: 2. Of those that a mesh axis runs over, the one named last changes fastest.
Arguments:
- tokens: bfloat16 [1024, 8, 1024], P('tp', 'rows'), may hold values from -6 to 6
- memory: bfloat16 [1024, 8, 1024], P('tp', 'rows'), may hold values from -6 to 6
- out_grad: bfloat16 [1024, 8, 1024], P('tp', 'rows'), may hold values from -6 to 6
- dec_segments: int32 [8, 1024], P('rows'), may hold values from 0 to 2, as said below
- src_segments: int32 [8, 1024], P('rows'), may hold values from 0 to 2, as said below
- self_query: bfloat16 [1024, 1024], P(None, 'tp'), may hold values from -0.1875 to 0.1875
- self_key: bfloat16 [1024, 1024], P(None, 'tp'), may hold values from -0.1875 to 0.1875
- self_value: bfloat16 [1024, 1024], P(None, 'tp'), may hold values from -0.1875 to 0.1875
- self_out: bfloat16 [1024, 1024], P('tp'), may hold values from -1.5 to 1.5
- cross_query: bfloat16 [1024, 1024], P(None, 'tp'), may hold values from -0.1875 to 0.1875
- cross_key: bfloat16 [1024, 1024], P(None, 'tp'), may hold values from -0.1875 to 0.1875
- cross_value: bfloat16 [1024, 1024], P(None, 'tp'), may hold values from -0.1875 to 0.1875
- cross_out: bfloat16 [1024, 1024], P('tp'), may hold values from -1.5 to 1.5
- ffn_in: bfloat16 [1024, 4096], P(None, 'tp'), may hold values from -0.1875 to 0.1875
- ffn_out: bfloat16 [4096, 1024], P('tp'), may hold values from -0.09375 to 0.09375
- adapt_down: bfloat16 [1024, 512], replicated, may hold values from -0.1875 to 0.1875
- adapt_down_bias: float32 [512], replicated, may hold values from -3 to 3
- adapt_up: bfloat16 [512, 1024], replicated, may hold values from -0.0625 to 0.0625
- adapt_up_bias: float32 [1024], replicated, may hold values from -0.6 to 0.6
- self_prefix: bfloat16 [2, 30, 1024], P(None, None, 'tp'), may hold values from -6 to 6
- cross_prefix: bfloat16 [2, 30, 1024], P(None, None, 'tp'), may hold values from -6 to 6
- norm_gain: float32 [3, 1024], replicated, may hold values from 0.5 to 1.5
- norm_shift: float32 [3, 1024], replicated, may hold values from -1.8 to 1.8
Outputs:
- output: bfloat16 [1024, 8, 1024], P('tp', 'rows')
- tokens_grad: bfloat16 [1024, 8, 1024], P('tp', 'rows')
- memory_grad: bfloat16 [1024, 8, 1024], P('tp', 'rows')
- self_prefix_grad: float32 [2, 30, 1024], P(None, None, 'tp')
- cross_prefix_grad: float32 [2, 30, 1024], P(None, None, 'tp')
- gain_grad: float32 [3, 1024], replicated
- shift_grad: float32 [3, 1024], replicated
- adapt_down_grad: float32 [1024, 512], replicated
- adapt_down_bias_grad: float32 [512], replicated
- adapt_up_grad: float32 [512, 1024], replicated
- adapt_up_bias_grad: float32 [1024], replicated
Inputs may be any that keep to these rules, and one draw needn't show every extreme that they name: `dec_segments`: each row holds documents 0, 1 and 2 in this order; document 1 begins at a position from 1 to 127 and ends among the last 128 positions, before the row's last position. `src_segments`: each row holds documents 0, 1 and 2 in this order; document 1 begins at a position from 1 to 127 and ends among the last 128 positions, before the row's last position.
All inputs are finite; a program needn't handle non-finite values.
Results may differ from a plain program's by a relative error of at most 0.025.
Values may be sent and summed in bfloat16 or wider, within the bound.
A program may use at most 192 MiB of HBM per device.

v0:
```python
import jax
import jax.numpy as jnp
from jax import lax
from jax.sharding import PartitionSpec as P

HEAD = 64


MASKED = -1000000000.0
EPSILON = 1e-05


def gelu_exact(value):
    return jax.nn.gelu(value, approximate=False)


def gelu_back(value, grad_out):
    return jax.vjp(gelu_exact, value)[1](grad_out)[0]


def layer_norm(value, gain, shift):
    centered = value - jnp.mean(value, axis=-1, keepdims=True)
    spread = lax.rsqrt(jnp.mean(centered * centered, axis=-1, keepdims=True) + EPSILON)
    return centered * spread * gain + shift


def product(left_side, right_side):
    return jnp.dot(left_side, right_side, preferred_element_type=jnp.float32)


def to_rows(array):
    return jnp.moveaxis(array, 1, 0)


def to_positions(array):
    return jnp.moveaxis(array, 0, 1)


def self_allowed(segments, prefix_len):
    position = jnp.arange(segments.shape[0])
    same_doc = (segments[:, None] == segments[None, :]) & (position[None, :] <= position[:, None])
    return jnp.concatenate(
        [jnp.ones((segments.shape[0], prefix_len), dtype=bool), same_doc], axis=1
    )


def cross_allowed(dec_row, src_row, prefix_len):
    same_doc = dec_row[:, None] == src_row[None, :]
    return jnp.concatenate([jnp.ones((dec_row.shape[0], prefix_len), dtype=bool), same_doc], axis=1)


def attend(queries, key_rows, value_rows, allowed):
    scores = jnp.einsum("qhd,khd->hqk", queries, key_rows, preferred_element_type=jnp.float32)
    scores = jnp.where(allowed[None], scores, MASKED)
    row_max = jnp.max(scores, axis=2, keepdims=True)
    exponent = jnp.exp(scores - row_max)
    row_total = jnp.sum(exponent, axis=2, keepdims=True)
    weights_low = (exponent / row_total).astype(jnp.bfloat16)
    mixture = jnp.einsum(
        "hqk,khd->qhd", weights_low, value_rows, preferred_element_type=jnp.float32
    )
    return (mixture.reshape(queries.shape[0], -1), (row_max + jnp.log(row_total))[:, :, 0])


def attend_back(queries, key_rows, value_rows, allowed, log_total, grad_mixed):
    scores = jnp.einsum("qhd,khd->hqk", queries, key_rows, preferred_element_type=jnp.float32)
    scores = jnp.where(allowed[None], scores, MASKED)
    probability = jnp.exp(scores - log_total[:, :, None])
    grad_heads = grad_mixed.reshape(queries.shape)
    grad_prob = jnp.einsum(
        "qhd,khd->hqk", grad_heads, value_rows, preferred_element_type=jnp.float32
    )
    row_delta = jnp.sum(probability * grad_prob, axis=2, keepdims=True)
    grad_score = (probability * (grad_prob - row_delta)).astype(jnp.bfloat16)
    grad_query = jnp.einsum(
        "hqk,khd->qhd", grad_score, key_rows, preferred_element_type=jnp.float32
    )
    grad_key = jnp.einsum("hqk,qhd->khd", grad_score, queries, preferred_element_type=jnp.float32)
    grad_value = jnp.einsum(
        "hqk,qhd->khd",
        probability.astype(jnp.bfloat16),
        grad_heads,
        preferred_element_type=jnp.float32,
    )
    return (grad_query, grad_key, grad_value)


def row_terms(left_side, right_side, row_count):
    return product(left_side.reshape(row_count, left_side.shape[2]), right_side)


def merge_heads(grad_heads):
    merged = grad_heads.astype(jnp.bfloat16).reshape(grad_heads.shape[0], grad_heads.shape[1], -1)
    return to_positions(merged)


def prefix_grads(grad_key, grad_value, prefix_len):
    key_part = jnp.sum(grad_key[:, :prefix_len], axis=0)
    value_part = jnp.sum(grad_value[:, :prefix_len], axis=0)
    return jnp.stack([key_part, value_part]).reshape(2, prefix_len, -1)


def per_device(
    tokens,
    memory,
    out_grad,
    dec_segments,
    src_segments,
    self_query,
    self_key,
    self_value,
    self_out,
    cross_query,
    cross_key,
    cross_value,
    cross_out,
    ffn_in,
    ffn_out,
    adapt_down,
    adapt_down_bias,
    adapt_up,
    adapt_up_bias,
    self_prefix,
    cross_prefix,
    norm_gain,
    norm_shift,
):
    seq_local, rows_local, width = tokens.shape
    head_local = self_query.shape[1] // HEAD
    prefix_len = self_prefix.shape[1]
    token_rows = seq_local * rows_local
    score_scale = HEAD ** (-0.5)
    local_shape = (seq_local, rows_local, width)
    gathered_tokens, gathered_memory = (
        lax.all_gather(tokens, "tp", axis=0, tiled=True),
        lax.all_gather(memory, "tp", axis=0, tiled=True),
    )
    seq_len = gathered_tokens.shape[0]

    def flatten(array):
        return array.reshape(seq_len * rows_local, array.shape[2])

    def split_heads(flat_values):
        return to_rows(
            flat_values.astype(jnp.bfloat16).reshape(seq_len, rows_local, head_local, HEAD)
        )

    self_pre = self_prefix.reshape(2, prefix_len, head_local, HEAD)
    cross_pre = cross_prefix.reshape(2, prefix_len, head_local, HEAD)
    tokens_flat = flatten(gathered_tokens)
    self_queries = split_heads(score_scale * product(tokens_flat, self_query))
    self_keys = split_heads(product(tokens_flat, self_key))
    self_values = split_heads(product(tokens_flat, self_value))

    def self_row(packed):
        queries, key_rows, value_rows, segments = packed
        return attend(
            queries,
            jnp.concatenate([self_pre[0], key_rows]),
            jnp.concatenate([self_pre[1], value_rows]),
            self_allowed(segments, prefix_len),
        )

    self_mixed, self_total = lax.map(self_row, (self_queries, self_keys, self_values, dec_segments))
    self_mixed = to_positions(self_mixed.astype(jnp.bfloat16))
    self_sum = lax.psum_scatter(
        row_terms(self_mixed, self_out, lax.axis_size("tp") * token_rows),
        "tp",
        scatter_dimension=0,
        tiled=True,
    )
    normed_one, norm_back_one = jax.vjp(
        layer_norm,
        tokens.astype(jnp.float32) + self_sum.reshape(local_shape),
        norm_gain[0],
        norm_shift[0],
    )
    gathered_one = lax.all_gather(normed_one.astype(jnp.bfloat16), "tp", axis=0, tiled=True)
    memory_flat = flatten(gathered_memory)
    cross_queries = split_heads(score_scale * product(flatten(gathered_one), cross_query))
    cross_keys = split_heads(product(memory_flat, cross_key))
    cross_values = split_heads(product(memory_flat, cross_value))

    def cross_row(packed):
        queries, key_rows, value_rows, dec_row, src_row = packed
        return attend(
            queries,
            jnp.concatenate([cross_pre[0], key_rows]),
            jnp.concatenate([cross_pre[1], value_rows]),
            cross_allowed(dec_row, src_row, prefix_len),
        )

    cross_mixed, cross_total = lax.map(
        cross_row, (cross_queries, cross_keys, cross_values, dec_segments, src_segments)
    )
    cross_mixed = to_positions(cross_mixed.astype(jnp.bfloat16))
    cross_sum = lax.psum_scatter(
        row_terms(cross_mixed, cross_out, token_rows * lax.axis_size("tp")).astype(jnp.bfloat16),
        "tp",
        scatter_dimension=0,
        tiled=True,
    ).astype(jnp.float32)
    normed_two, norm_back_two = jax.vjp(
        layer_norm, normed_one + cross_sum.reshape(local_shape), norm_gain[1], norm_shift[1]
    )
    normed_low = normed_two.astype(jnp.bfloat16)
    own_rows = normed_low.reshape(token_rows, width)
    normed_flat = flatten(lax.all_gather(normed_low, "tp", axis=0, tiled=True))
    hidden = gelu_exact(product(normed_flat, ffn_in)).astype(jnp.bfloat16)
    ffn_sum = lax.psum_scatter(
        row_terms(
            hidden.reshape(seq_len, rows_local, -1), ffn_out, token_rows * lax.axis_size("tp")
        ).astype(jnp.bfloat16),
        "tp",
        scatter_dimension=0,
        tiled=True,
    ).astype(jnp.float32)
    adapt_pre = product(own_rows, adapt_down) + adapt_down_bias
    adapt_act = gelu_exact(adapt_pre).astype(jnp.bfloat16)
    adapt_sum = product(adapt_act, adapt_up) + adapt_up_bias
    residual = normed_two + (ffn_sum + 4.0 * adapt_sum).reshape(local_shape)
    mixed_out, norm_back_three = jax.vjp(layer_norm, residual, norm_gain[2], norm_shift[2])
    output = mixed_out.astype(jnp.bfloat16)
    grad_resid, gain_three, shift_three = norm_back_three(out_grad.astype(jnp.float32))
    grad_low = grad_resid.astype(jnp.bfloat16)
    grad_four = (4.0 * grad_resid).astype(jnp.bfloat16).reshape(token_rows, width)
    adapt_up_part = product(adapt_act.T, grad_four)
    adapt_up_bias_part = jnp.sum(grad_four.astype(jnp.float32), axis=0)
    grad_adapt = gelu_back(adapt_pre, product(grad_four, adapt_up.T)).astype(jnp.bfloat16)
    adapt_down_part = product(own_rows.T, grad_adapt)
    adapt_down_bias_part = jnp.sum(grad_adapt.astype(jnp.float32), axis=0)
    grad_normed = grad_resid + product(grad_adapt, adapt_down.T).reshape(local_shape)
    grad_flat = flatten(lax.all_gather(grad_low, "tp", axis=0, tiled=True))
    grad_hidden = gelu_back(product(normed_flat, ffn_in), product(grad_flat, ffn_out.T)).astype(
        jnp.bfloat16
    )
    ffn_back_sum = lax.psum_scatter(
        row_terms(
            grad_hidden.reshape(seq_len, rows_local, -1), ffn_in.T, token_rows * lax.axis_size("tp")
        ).astype(jnp.bfloat16),
        "tp",
        scatter_dimension=0,
        tiled=True,
    ).astype(jnp.float32)
    grad_normed = grad_normed + ffn_back_sum.reshape(local_shape)
    grad_two, gain_two, shift_two = norm_back_two(grad_normed)
    cross_grad_flat = flatten(
        lax.all_gather(grad_two.astype(jnp.bfloat16), "tp", axis=0, tiled=True)
    )
    cross_grad_mixed = to_rows(
        product(cross_grad_flat, cross_out.T).astype(jnp.bfloat16).reshape(seq_len, rows_local, -1)
    )

    def cross_row_back(packed):
        queries, key_rows, value_rows, dec_row, src_row, log_total, grad_mixed = packed
        return attend_back(
            queries,
            jnp.concatenate([cross_pre[0], key_rows]),
            jnp.concatenate([cross_pre[1], value_rows]),
            cross_allowed(dec_row, src_row, prefix_len),
            log_total,
            grad_mixed,
        )

    cross_dq, cross_dk, cross_dv = lax.map(
        cross_row_back,
        (
            cross_queries,
            cross_keys,
            cross_values,
            dec_segments,
            src_segments,
            cross_total,
            cross_grad_mixed,
        ),
    )
    cross_prefix_part = prefix_grads(cross_dk, cross_dv, prefix_len)
    cross_query_grad = merge_heads(cross_dq)
    memory_key_grad = merge_heads(cross_dk[:, prefix_len:])
    memory_value_grad = merge_heads(cross_dv[:, prefix_len:])
    pieces = [
        array.reshape(token_rows * lax.axis_size("tp"), -1)
        for array in (cross_query_grad, memory_key_grad, memory_value_grad)
    ]
    to_query = score_scale * product(pieces[0], cross_query.T)
    to_memory = product(pieces[1], cross_key.T) + product(pieces[2], cross_value.T)
    both_grads = lax.psum_scatter(
        jnp.concatenate([to_query, to_memory], axis=1).astype(jnp.bfloat16),
        "tp",
        scatter_dimension=0,
        tiled=True,
    ).astype(jnp.float32)
    memory_grad = both_grads[:, width:].reshape(local_shape).astype(jnp.bfloat16)
    grad_one, gain_one, shift_one = norm_back_one(
        grad_two + both_grads[:, :width].reshape(local_shape)
    )
    self_grad_flat = flatten(
        lax.all_gather(grad_one.astype(jnp.bfloat16), "tp", axis=0, tiled=True)
    )
    self_grad_mixed = to_rows(
        product(self_grad_flat, self_out.T).astype(jnp.bfloat16).reshape(seq_len, rows_local, -1)
    )

    def self_row_back(packed):
        queries, key_rows, value_rows, segments, log_total, grad_mixed = packed
        return attend_back(
            queries,
            jnp.concatenate([self_pre[0], key_rows]),
            jnp.concatenate([self_pre[1], value_rows]),
            self_allowed(segments, prefix_len),
            log_total,
            grad_mixed,
        )

    self_dq, self_dk, self_dv = lax.map(
        self_row_back,
        (self_queries, self_keys, self_values, dec_segments, self_total, self_grad_mixed),
    )
    self_prefix_part = prefix_grads(self_dk, self_dv, prefix_len)
    self_query_grad = merge_heads(self_dq)
    self_key_grad = merge_heads(self_dk[:, prefix_len:])
    self_value_grad = merge_heads(self_dv[:, prefix_len:])
    pieces = [
        array.reshape(token_rows * lax.axis_size("tp"), -1)
        for array in (self_query_grad, self_key_grad, self_value_grad)
    ]
    self_input_sum = lax.psum_scatter(
        (
            score_scale * product(pieces[0], self_query.T)
            + product(pieces[1], self_key.T)
            + product(pieces[2], self_value.T)
        ).astype(jnp.bfloat16),
        "tp",
        scatter_dimension=0,
        tiled=True,
    ).astype(jnp.float32)
    tokens_grad = (grad_one + self_input_sum.reshape(local_shape)).astype(jnp.bfloat16)
    self_prefix_grad, cross_prefix_grad = lax.psum((self_prefix_part, cross_prefix_part), "rows")
    (
        gain_grad,
        shift_grad,
        adapt_down_grad,
        adapt_down_bias_grad,
        adapt_up_grad,
        adapt_up_bias_grad,
    ) = lax.psum(
        (
            jnp.stack([gain_one, gain_two, gain_three]),
            jnp.stack([shift_one, shift_two, shift_three]),
            adapt_down_part,
            adapt_down_bias_part,
            adapt_up_part,
            adapt_up_bias_part,
        ),
        ("rows", "tp"),
    )
    return (
        output,
        tokens_grad,
        memory_grad,
        self_prefix_grad,
        cross_prefix_grad,
        gain_grad,
        shift_grad,
        adapt_down_grad,
        adapt_down_bias_grad,
        adapt_up_grad,
        adapt_up_bias_grad,
    )


def solution(mesh):
    placed = (
        P("tp", "rows", None),
        P("tp", "rows", None),
        P("tp", "rows", None),
        P("rows", None),
        P("rows", None),
        P(None, "tp"),
        P(None, "tp"),
        P(None, "tp"),
        P("tp", None),
        P(None, "tp"),
        P(None, "tp"),
        P(None, "tp"),
        P("tp", None),
        P(None, "tp"),
        P("tp", None),
        P(),
        P(),
        P(),
        P(),
        P(None, None, "tp"),
        P(None, None, "tp"),
        P(),
        P(),
    )
    return jax.shard_map(
        per_device,
        mesh=mesh,
        in_specs=placed,
        out_specs=(
            P("tp", "rows", None),
            P("tp", "rows", None),
            P("tp", "rows", None),
            P(None, None, "tp"),
            P(None, None, "tp"),
            P(),
            P(),
            P(),
            P(),
            P(),
            P(),
        ),
        check_vma=False,
    )
```

profile of v0, /device:TPU:0, one launch (start us, length us, event | category | flops | bytes accessed | tf_op | source)
XLA Modules:
  0.0 823.7 jit_solution(13568950078421503958)
XLA Ops:
  9.2 3.1 broadcast_compare_fusion
  12.9 22.0 %all-gather.8.cloned.1.call-done = bf16[1024,1,1024]{2,0,1:T(8,128)(2,1)} async-done(((bf16[256,1,1024]{2,0,1:T(8,128)(2,1)}), bf16[1024,1,1024]{2,0,1:T(8,128)(2,1)}) %all-gather.8.cloned.1.call-update) | async-done | bytes 2097168 | tf_op jit(solution)/shard_map/all_gather | solution.py:135
  34.9 2.4 fusion.85
  37.4 2.6 fusion.67
  40.0 8.1 fusion.136
  48.1 8.4 %fusion = f32[4,1024]{1,0:T(4,128)S(1)} fusion(f32[4,1024,1054]{1,2,0:T(8,128)} %get-tuple-element.178, f32[4,1024]{1,0:T(4,128)S(1)} %get-tuple-element.177), kind=kLoop, calls=%fused_computation.12 | loop fusion | flops 8630272 | bytes 17301504 | tf_op jit(solution)/shard_map/while/body/eval_jaxpr/reduce_sum | solution.py:57
  57.3 9.3 %fusion.89 = bf16[4,64,1024]{2,1,0:T(8,128)(2,1)S(1)} fusion(f32[4,1024,1054]{1,2,0:T(8,128)} %get-tuple-element.178, f32[4,1024]{1,0:T(4,128)S(1)} %fusion, f32[4,1024]{1,0:T(4,128)S(1)} %get-tuple-element.177, bf16[1024,4,64]{0,2,1:T(8,128)(2,1)S(1)} %bitcast.245, bf16[30,4,64]{0,2,1:T(8,128)(2,1)S(1)} %bitcast.250), kind=kOutput, calls=%fused_computation.102 | convolution fusion | flops 566892544 | bytes 18365440 | tf_op jit(solution)/shard_map/while/body/eval_jaxpr/hqk,khd->qhd/dot_general | solution.py:59
  66.7 2.8 fusion.139
  70.6 43.5 %reduce-scatter.7.cloned.1.call-done = f32[256,1024]{1,0:T(8,128)} async-done(((f32[1024,1024]{1,0:T(8,128)}), f32[256,1024]{1,0:T(8,128)}) %reduce-scatter.7.cloned.1.call-update) | async-done | bytes 1048592 | tf_op jit(solution)/shard_map/reduce_scatter | solution.py:166
  117.3 2.9 concatenate.46
  120.3 18.0 %all-gather.10.cloned.1.call-done = bf16[1024,1,1024]{2,0,1:T(8,128)(2,1)} async-done(((bf16[256,1,1024]{2,0,1:T(8,128)(2,1)}), bf16[1024,1,1024]{2,0,1:T(8,128)(2,1)}) %all-gather.10.cloned.1.call-update) | async-done | bytes 2097168 | tf_op jit(solution)/shard_map/all_gather | solution.py:136
  138.4 3.2 fusion.73
  141.6 3.2 fusion.70
  144.8 18.3 %all-gather.12.cloned.1.call-done = bf16[1024,1,1024]{2,0,1:T(8,128)(2,1)} async-done(((bf16[256,1,1024]{2,0,1:T(8,128)(2,1)}), bf16[1024,1,1024]{2,0,1:T(8,128)(2,1)}) %all-gather.12.cloned.1.call-update) | async-done | bytes 2097168 | tf_op jit(solution)/shard_map/all_gather | solution.py:178
  163.1 2.5 fusion.82
  165.6 9.3 %fusion.137 = (f32[4,1024]{1,0:T(4,128)S(1)}, f32[4,1024,1054]{1,2,0:T(8,128)}) fusion(bf16[1024,4,64]{0,2,1:T(8,128)(2,1)S(1)} %bitcast.220, bf16[1024,4,64]{0,2,1:T(8,128)(2,1)} %bitcast.232, bf16[30,4,64]{0,2,1:T(8,128)(2,1)S(1)} %bitcast.243, pred[1024,1054]{0,1:T(8,128)(4,1)S(1)} %copy-done.8), kind=kOutput, calls=%fused_computation.208 | convolution fusion | flops 562309120 | bytes 19428352 | tf_op jit(solution)/shard_map/while/body/eval_jaxpr/qhd,khd->hqk/dot_general | solution.py:53
  174.9 8.3 %fusion.1 = f32[4,1024]{1,0:T(4,128)S(1)} fusion(f32[4,1024,1054]{1,2,0:T(8,128)} %get-tuple-element.180, f32[4,1024]{1,0:T(4,128)S(1)} %get-tuple-element.179), kind=kLoop, calls=%fused_computation.13 | loop fusion | flops 8630272 | bytes 17301504 | tf_op jit(solution)/shard_map/while/body/eval_jaxpr/reduce_sum | solution.py:57
  183.2 9.2 %fusion.88 = bf16[4,64,1024]{2,1,0:T(8,128)(2,1)S(1)} fusion(f32[4,1024,1054]{1,2,0:T(8,128)} %get-tuple-element.180, f32[4,1024]{1,0:T(4,128)S(1)} %fusion.1, f32[4,1024]{1,0:T(4,128)S(1)} %get-tuple-element.179, bf16[1024,4,64]{0,2,1:T(8,128)(2,1)S(1)} %bitcast.248, bf16[30,4,64]{0,2,1:T(8,128)(2,1)S(1)} %bitcast.252), kind=kOutput, calls=%fused_computation.101 | convolution fusion | flops 566892544 | bytes 18365440 | tf_op jit(solution)/shard_map/while/body/eval_jaxpr/hqk,khd->qhd/dot_general | solution.py:59
  192.4 2.1 convolution_convert_fusion.1
  194.5 10.4 %all-gather.14.cloned.1.call-start = ((), (), s32[]{:S(2)}) async-start(), calls=%async_computation.11 | async-start | bytes 2621440 | tf_op jit(solution)/shard_map/all_gather | solution.py:208
  204.9 21.2 %reduce-scatter.9.cloned.1.call-done = bf16[256,1024]{1,0:T(8,128)(2,1)} async-done(((bf16[1024,1024]{1,0:T(8,128)(2,1)}), bf16[256,1024]{1,0:T(8,128)(2,1)}) %reduce-scatter.9.cloned.1.call-update) | async-done | bytes 524304 | tf_op jit(solution)/shard_map/reduce_scatter | solution.py:197
  229.6 22.7 %all-gather.14.cloned.1.call-done = bf16[1024,1,1024]{2,0,1:T(8,128)(2,1)} async-done(((bf16[256,1,1024]{2,0,1:T(8,128)(2,1)}), bf16[1024,1,1024]{2,0,1:T(8,128)(2,1)}) %all-gather.14.cloned.1.call-update) | async-done | bytes 2097168 | tf_op jit(solution)/shard_map/all_gather | solution.py:208
  252.3 12.2 %fusion.12 = (f32[1024,1024]{1,0:T(8,128)S(1)}, f32[1024,1024]{1,0:T(8,128)S(1)}) fusion(bf16[1024,1024]{1,0:T(8,128)(2,1)S(1)} %copy-done, bf16[1024,1,1024]{2,0,1:T(8,128)(2,1)} %all-gather.14.cloned.1.call-done), kind=kOutput, calls=%fused_computation.23 | convolution fusion | flops 2212495360 | bytes 12582912 | tf_op jit(solution)/shard_map/dot_general | solution.py:28
  264.6 1.9 copy-done.71
  267.9 3.7 fusion.49
  271.7 3.9 multiply_convert_fusion.8
  275.6 27.6 %reduce-scatter.11.cloned.1.call-done = bf16[256,1024]{1,0:T(8,128)(2,1)} async-done(((bf16[1024,1024]{1,0:T(8,128)(2,1)}), bf16[256,1024]{1,0:T(8,128)(2,1)}) %reduce-scatter.11.cloned.1.call-update) | async-done | bytes 524304 | tf_op jit(solution)/shard_map/reduce_scatter | solution.py:210
  303.2 2.1 fusion.138
  309.2 22.7 %all-gather.16.cloned.1.call-done = bf16[1024,1,1024]{2,0,1:T(8,128)(2,1)} async-done(((bf16[256,1,1024]{2,0,1:T(8,128)(2,1)}), bf16[1024,1,1024]{2,0,1:T(8,128)(2,1)}) %all-gather.16.cloned.1.call-update) | async-done | bytes 2097168 | tf_op jit(solution)/shard_map/all_gather | solution.py:233
  331.9 10.7 %convolution_convert_fusion = bf16[1024,1024]{1,0:T(8,128)(2,1)} fusion(bf16[1024,1024]{1,0:T(8,128)(2,1)S(1)} %copy-done, f32[1024,1024]{1,0:T(8,128)} %copy-done.71, f32[1024,1024]{1,0:T(8,128)} %copy-done.72, bf16[1024,1024]{1,0:T(8,128)(2,1)} %param.37, bf16[1024,1,1024]{2,0,1:T(8,128)(2,1)} %all-gather.16.cloned.1.call-done), kind=kOutput, calls=%fused_computation.73 | convolution fusion | flops 4310695936 | bytes 16777216 | tf_op jit(solution)/shard_map/dot_general | solution.py:28
  342.7 2.1 convert_reduce_fusion.1
  344.8 2.9 convert_reduce_fusion.2
  347.7 26.5 %reduce-scatter.13.cloned.1.call-done = bf16[256,1024]{1,0:T(8,128)(2,1)} async-done(((bf16[1024,1024]{1,0:T(8,128)(2,1)}), bf16[256,1024]{1,0:T(8,128)(2,1)}) %reduce-scatter.13.cloned.1.call-update) | async-done | bytes 524304 | tf_op jit(solution)/shard_map/reduce_scatter | solution.py:237
  374.2 2.7 multiply_reduce_fusion.2
  378.8 22.3 %all-gather.18.cloned.1.call-done = bf16[1024,1,1024]{2,0,1:T(8,128)(2,1)} async-done(((bf16[256,1,1024]{2,0,1:T(8,128)(2,1)}), bf16[1024,1,1024]{2,0,1:T(8,128)(2,1)}) %all-gather.18.cloned.1.call-update) | async-done | bytes 2097168 | tf_op jit(solution)/shard_map/all_gather | solution.py:248
  401.1 2.6 fusion.76
  403.7 14.2 %multiply_reduce_fusion.1 = (f32[4,1024]{1,0:T(4,128)S(1)}, f32[4,1024,1054]{1,2,0:T(8,128)}) fusion(f32[4,1024,1054]{1,2,0:T(8,128)} %get-tuple-element.180, f32[4,1024]{1,0:T(4,128)S(1)} %log_add_fusion.1, bf16[1024,4,64]{0,2,1:T(8,128)(2,1)S(1)} %bitcast.224, bf16[1024,4,64]{0,2,1:T(8,128)(2,1)} %bitcast.247, bf16[30,4,64]{0,2,1:T(8,128)(2,1)S(1)} %bitcast.253), kind=kOutput, calls=%fused_computation.6 | convolution fusion | flops 566626304 | bytes 35634176 | tf_op jit(solution)/shard_map/while/body/eval_jaxpr/qhd,khd->hqk/dot_general | solution.py:70
  419.4 3.8 fusion.19
  423.3 8.0 multiply_convert_fusion.1
  431.4 2.8 convolution_bitcast_fusion.1
  434.2 1.8 convolution_convert_fusion.3
  439.1 2.5 pad_maximum_fusion
  441.8 44.4 %reduce-scatter.15.cloned.1.call-done = bf16[256,2048]{1,0:T(8,128)(2,1)} async-done(((bf16[1024,2048]{1,0:T(8,128)(2,1)}), bf16[256,2048]{1,0:T(8,128)(2,1)}) %reduce-scatter.15.cloned.1.call-update) | async-done | bytes 1048592 | tf_op jit(solution)/shard_map/reduce_scatter | solution.py:287
  486.2 2.2 multiply_reduce_fusion.3
  488.4 1.6 fusion.126
  492.0 22.7 %all-gather.20.cloned.1.call-done = bf16[1024,1,1024]{2,0,1:T(8,128)(2,1)} async-done(((bf16[256,1,1024]{2,0,1:T(8,128)(2,1)}), bf16[1024,1,1024]{2,0,1:T(8,128)(2,1)}) %all-gather.20.cloned.1.call-update) | async-done | bytes 2097168 | tf_op jit(solution)/shard_map/all_gather | solution.py:298
  514.6 2.3 fusion.79
  517.1 15.8 %multiply_reduce_fusion = (f32[4,1024]{1,0:T(4,128)S(1)}, f32[4,1024,1054]{1,2,0:T(8,128)}) fusion(f32[4,1024,1054]{1,2,0:T(8,128)} %get-tuple-element.178, f32[4,1024]{1,0:T(4,128)S(1)} %log_add_fusion, bf16[1024,4,64]{0,2,1:T(8,128)(2,1)S(1)} %bitcast.222, bf16[1024,4,64]{0,2,1:T(8,128)(2,1)S(1)} %bitcast.246, bf16[30,4,64]{0,2,1:T(8,128)(2,1)S(1)} %bitcast.251), kind=kOutput, calls=%fused_computation.3 | convolution fusion | flops 566626304 | bytes 35634176 | tf_op jit(solution)/shard_map/while/body/eval_jaxpr/qhd,khd->hqk/dot_general | solution.py:70
  533.2 8.0 multiply_convert_fusion
  541.3 2.8 convolution_bitcast_fusion
  544.1 4.0 convolution_convert_fusion.2
  548.1 3.8 fusion.22
  552.2 1.9 fusion.142
  555.1 2.1 add_convert_fusion
  557.5 1.8 fusion.99
  559.4 1.8 fusion.143
  561.6 40.4 %all-reduce.2 = (f32[3,1024]{1,0:T(4,128)}, f32[3,1024]{1,0:T(4,128)}, f32[512]{0:T(512)}, f32[1024]{0:T(1024)}) all-reduce(f32[3,1024]{1,0:T(4,128)S(1)} %get-tuple-element.193, f32[3,1024]{1,0:T(4,128)S(1)} %get-tuple-element.194, f32[512]{0:T(512)S(1)} %copy-done.66, ...), channel_id=1, replica_groups=mesh['rows'=8,'tp'=4] {'rows','tp'}, use_global_device_ids=true, to_apply=%region_29.30 | all-reduce | flops 7680 | bytes 61440 | tf_op jit(solution)/shard_map/psum | solution.py:346
  602.0 1.9 slice_bitcast_fusion
  604.9 2.0 fusion.94
  606.9 130.2 %all-reduce.8.cloned.1.call-done = (f32[1024,512]{1,0:T(8,128)}, f32[512,1024]{1,0:T(8,128)}) async-done(((f32[1024,512]{1,0:T(8,128)}, f32[512,1024]{1,0:T(8,128)}), (f32[1024,512]{1,0:T(8,128)}, f32[512,1024]{1,0:T(8,128)})) %all-reduce.8.cloned.1.call-update) | async-done | bytes 4194320 | tf_op jit(solution)/shard_map/psum | solution.py:346
  737.1 72.2 %all-reduce.10.cloned.1.call-done = (f32[2,30,256]{2,0,1:T(2,128)}, f32[2,30,256]{2,0,1:T(2,128)}) async-done(((f32[2,30,256]{2,0,1:T(2,128)}, f32[2,30,256]{2,0,1:T(2,128)}), (f32[2,30,256]{2,0,1:T(2,128)}, f32[2,30,256]{2,0,1:T(2,128)})) %all-reduce.10.cloned.1.call-update) | async-done | bytes 122896 | tf_op jit(solution)/shard_map/psum | solution.py:338
  809.4 1.6 copy.52
  811.0 1.6 copy.53
  812.6 3.1 copy.54
  (257 shorter events, 29.8 us)
Async XLA Ops:
  7.2 245.2 %copy-start = (bf16[1024,1024]{1,0:T(8,128)(2,1)S(1)}, bf16[1024,1024]{1,0:T(8,128)(2,1)}, u32[]{:S(2)}) copy-start(bf16[1024,1024]{1,0:T(8,128)(2,1)} %param.36) | copy-start | bytes 6291460
  7.2 27.7 %all-gather.8.cloned.1.call-start = ((), (), s32[]{:S(2)}) async-start(), calls=%async_computation.6 | async-start | bytes 2621440 | tf_op jit(solution)/shard_map/all_gather | solution.py:135
  7.9 106.2 %reduce-scatter.7.cloned.1.call-start = ((), (), s32[]{:S(2)}) async-start(), calls=%async_computation.7 | async-start | bytes 5242880 | tf_op jit(solution)/shard_map/reduce_scatter | solution.py:166
  9.0 31.0 %copy-start.29 = (bf16[1,30,256]{1,2,0:T(8,128)(2,1)}, bf16[1,30,256]{1,2,0:T(8,128)(2,1)S(1)}, u32[]{:S(2)}) copy-start(bf16[1,30,256]{1,2,0:T(8,128)(2,1)S(1)} %copy.35) | copy-start | bytes 46084
  9.2 48.1 %copy-start.45 = (bf16[1,30,256]{1,2,0:T(8,128)(2,1)}, bf16[1,30,256]{1,2,0:T(8,128)(2,1)S(1)}, u32[]{:S(2)}) copy-start(bf16[1,30,256]{1,2,0:T(8,128)(2,1)S(1)} %copy.34) | copy-start | bytes 46084
  37.3 10.7 %copy-start.12 = (bf16[1024,256]{0,1:T(8,128)(2,1)}, bf16[1024,256]{0,1:T(8,128)(2,1)S(1)}, u32[]{:S(2)}) copy-start(bf16[1024,256]{0,1:T(8,128)(2,1)S(1)} %fusion.85) | copy-start | bytes 1572868
  40.0 8.1 copy-start.20
  48.1 9.2 %copy-start.51 = (f32[4,1024]{1,0:T(4,128)}, f32[4,1024]{1,0:T(4,128)S(1)}, u32[]{:S(2)}) copy-start(f32[4,1024]{1,0:T(4,128)S(1)} %get-tuple-element.177) | copy-start | bytes 49156
  48.1 8.4 %copy-start.41 = (bf16[1024,256]{1,0:T(8,128)(2,1)S(1)}, bf16[1024,256]{1,0:T(8,128)(2,1)}, u32[]{:S(2)}) copy-start(bf16[1024,256]{1,0:T(8,128)(2,1)} %param.30) | copy-start | bytes 1572868
  48.1 8.4 %copy-start.68 = (bf16[1024,1,1024]{2,0,1:T(8,128)(2,1)S(1)}, bf16[1024,1,1024]{2,0,1:T(8,128)(2,1)}, u32[]{:S(2)}) copy-start(bf16[1024,1,1024]{2,0,1:T(8,128)(2,1)} %all-gather.8.cloned.1.call-done) | copy-start | bytes 6291460
  56.5 10.1 %copy-start.54 = (f32[4,1024]{1,0:T(4,128)}, f32[4,1024]{1,0:T(4,128)S(1)}, u32[]{:S(2)}) copy-start(f32[4,1024]{1,0:T(4,128)S(1)} %fusion) | copy-start | bytes 49156
  57.3 9.4 %copy-start.33 = (bf16[1024,256]{0,1:T(8,128)(2,1)}, bf16[1024,256]{0,1:T(8,128)(2,1)S(1)}, u32[]{:S(2)}) copy-start(bf16[1024,256]{0,1:T(8,128)(2,1)S(1)} %fusion.64) | copy-start | bytes 1572868
  57.3 9.3 %copy-start.38 = (bf16[256,1024]{1,0:T(8,128)(2,1)S(1)}, bf16[256,1024]{1,0:T(8,128)(2,1)}, u32[]{:S(2)}) copy-start(bf16[256,1024]{1,0:T(8,128)(2,1)} %param.31) | copy-start | bytes 1572868
  69.4 47.6 %copy-start.53 = (bf16[2,30,256]{2,0,1:T(2,128)(2,1)S(1)}, bf16[2,30,256]{2,0,1:T(2,128)(2,1)}, u32[]{:S(2)}) copy-start(bf16[2,30,256]{2,0,1:T(2,128)(2,1)} %param.43) | copy-start | bytes 92164
  69.5 68.9 %all-gather.10.cloned.1.call-start = ((), (), s32[]{:S(2)}) async-start(), calls=%async_computation.8 | async-start | bytes 2621440 | tf_op jit(solution)/shard_map/all_gather | solution.py:136
  70.2 92.9 %all-gather.12.cloned.1.call-start = ((), (), s32[]{:S(2)}) async-start(), calls=%async_computation.9 | async-start | bytes 2621440 | tf_op jit(solution)/shard_map/all_gather | solution.py:178
  115.6 110.5 %copy-start.2 = (f32[256,1,1024]{2,0,1:T(8,128)}, f32[256,1,1024]{2,0,1:T(8,128)S(1)}, u32[]{:S(2)}) copy-start(f32[256,1,1024]{2,0,1:T(8,128)S(1)} %get-tuple-element.163) | copy-start | bytes 3145732
  115.9 28.9 %copy-start.64 = (f32[256]{0:T(256)}, f32[256]{0:T(256)S(1)}, u32[]{:S(2)}) copy-start(f32[256]{0:T(256)S(1)} %multiply_reduce_fusion.8) | copy-start | bytes 3076
  117.0 109.1 %reduce-scatter.9.cloned.1.call-start = ((), (), s32[]{:S(2)}) async-start(), calls=%async_computation.10 | async-start | bytes 2621440 | tf_op jit(solution)/shard_map/reduce_scatter | solution.py:197
  117.3 48.3 %copy-start.31 = (bf16[1,30,256]{1,2,0:T(8,128)(2,1)}, bf16[1,30,256]{1,2,0:T(8,128)(2,1)S(1)}, u32[]{:S(2)}) copy-start(bf16[1,30,256]{1,2,0:T(8,128)(2,1)S(1)} %copy.37) | copy-start | bytes 46084
  120.3 62.9 %copy-start.47 = (bf16[1,30,256]{1,2,0:T(8,128)(2,1)}, bf16[1,30,256]{1,2,0:T(8,128)(2,1)S(1)}, u32[]{:S(2)}) copy-start(bf16[1,30,256]{1,2,0:T(8,128)(2,1)S(1)} %copy.36) | copy-start | bytes 46084
  165.6 9.4 %copy-start.14 = (bf16[1024,256]{0,1:T(8,128)(2,1)}, bf16[1024,256]{0,1:T(8,128)(2,1)S(1)}, u32[]{:S(2)}) copy-start(bf16[1024,256]{0,1:T(8,128)(2,1)S(1)} %fusion.82) | copy-start | bytes 1572868
  174.9 8.3 %copy-start.35 = (bf16[1024,256]{0,1:T(8,128)(2,1)S(1)}, bf16[1024,256]{0,1:T(8,128)(2,1)}, u32[]{:S(2)}) copy-start(bf16[1024,256]{0,1:T(8,128)(2,1)} %fusion.70) | copy-start | bytes 1572868
  183.2 9.2 %copy-start.43 = (bf16[256,1024]{1,0:T(8,128)(2,1)S(1)}, bf16[256,1024]{1,0:T(8,128)(2,1)}, u32[]{:S(2)}) copy-start(bf16[256,1024]{1,0:T(8,128)(2,1)} %param.35) | copy-start | bytes 1572868
  194.5 57.8 %all-gather.14.cloned.1.call-start = ((), (), s32[]{:S(2)}) async-start(), calls=%async_computation.11 | async-start | bytes 2621440 | tf_op jit(solution)/shard_map/all_gather | solution.py:208
  229.6 73.6 %reduce-scatter.11.cloned.1.call-start = ((), (), s32[]{:S(2)}) async-start(), calls=%async_computation.12 | async-start | bytes 2621440 | tf_op jit(solution)/shard_map/reduce_scatter | solution.py:210
  252.3 15.6 %copy-start.67 = (bf16[1024,1024]{1,0:T(8,128)(2,1)S(1)}, bf16[1024,1024]{1,0:T(8,128)(2,1)}, u32[]{:S(2)}) copy-start(bf16[1024,1024]{1,0:T(8,128)(2,1)} %param.37) | copy-start | bytes 6291460
  271.6 31.6 %copy-start.5 = (f32[256,1,1024]{2,0,1:T(8,128)S(1)}, f32[256,1,1024]{2,0,1:T(8,128)}, u32[]{:S(2)}) copy-start(f32[256,1,1024]{2,0,1:T(8,128)} %copy-done.4) | copy-start | bytes 3145732
  271.6 31.6 %copy-start.69 = (f32[1024]{0:T(1024)S(1)}, f32[1024]{0:T(1024)}, u32[]{:S(2)}) copy-start(f32[1024]{0:T(1024)} %param.41) | copy-start | bytes 12292
  271.6 60.3 %all-gather.16.cloned.1.call-start = ((), (), s32[]{:S(2)}) async-start(), calls=%async_computation.13 | async-start | bytes 2621440 | tf_op jit(solution)/shard_map/all_gather | solution.py:233
  275.6 31.6 %copy-start.49 = (bf16[256,512]{1,0:T(8,128)(2,1)}, bf16[256,512]{1,0:T(8,128)(2,1)S(1)}, u32[]{:S(2)}) copy-start(bf16[256,512]{1,0:T(8,128)(2,1)S(1)} %get-tuple-element.147) | copy-start | bytes 786436
  309.2 65.1 %reduce-scatter.13.cloned.1.call-start = ((), (), s32[]{:S(2)}) async-start(), calls=%async_computation.14 | async-start | bytes 2621440 | tf_op jit(solution)/shard_map/reduce_scatter | solution.py:237
  342.6 31.6 %copy-start.7 = (f32[256,1,1024]{2,0,1:T(8,128)S(1)}, f32[256,1,1024]{2,0,1:T(8,128)}, u32[]{:S(2)}) copy-start(f32[256,1,1024]{2,0,1:T(8,128)} %copy-done.6) | copy-start | bytes 3145732
  342.6 58.4 %all-gather.18.cloned.1.call-start = ((), (), s32[]{:S(2)}) async-start(), calls=%async_computation.15 | async-start | bytes 2621440 | tf_op jit(solution)/shard_map/all_gather | solution.py:248
  344.8 32.2 %copy-start.25 = (bf16[256,1024]{1,0:T(8,128)(2,1)}, bf16[256,1024]{1,0:T(8,128)(2,1)S(1)}, u32[]{:S(2)}) copy-start(bf16[256,1024]{1,0:T(8,128)(2,1)S(1)} %get-tuple-element.138) | copy-start | bytes 1572868
  347.7 29.3 %copy-start.27 = (bf16[256,512]{1,0:T(8,128)(2,1)}, bf16[256,512]{1,0:T(8,128)(2,1)S(1)}, u32[]{:S(2)}) copy-start(bf16[256,512]{1,0:T(8,128)(2,1)S(1)} %get-tuple-element.140) | copy-start | bytes 786436
  377.4 26.3 %copy-start.48 = (bf16[1,30,256]{1,2,0:T(8,128)(2,1)S(1)}, bf16[1,30,256]{1,2,0:T(8,128)(2,1)}, u32[]{:S(2)}) copy-start(bf16[1,30,256]{1,2,0:T(8,128)(2,1)} %copy-done.47) | copy-start | bytes 46084
  377.4 26.3 %copy-start.60 = (f32[256]{0:T(256)}, f32[256]{0:T(256)S(1)}, u32[]{:S(2)}) copy-start(f32[256]{0:T(256)S(1)} %negate_multiply_fusion.3) | copy-start | bytes 3076
  378.3 107.9 %reduce-scatter.15.cloned.1.call-start = ((), (), s32[]{:S(2)}) async-start(), calls=%async_computation.16 | async-start | bytes 5242880 | tf_op jit(solution)/shard_map/reduce_scatter | solution.py:287
  401.1 16.8 %slice-start.5 = ((s8[17301504]{0:T(1024)(128)(4,1)}), s8[4194304]{0:T(1024)(128)(4,1)S(1)}, s32[]{:S(2)}) async-start(s8[17301504]{0:T(1024)(128)(4,1)} %bitcast.216), calls=%async_computation.26 | async-start | bytes 8388608
  403.7 14.2 %slice-start.6 = ((s8[17301504]{0:T(1024)(128)(4,1)}), s8[4194304]{0:T(1024)(128)(4,1)S(1)}, s32[]{:S(2)}) async-start(s8[17301504]{0:T(1024)(128)(4,1)} %bitcast.216), calls=%async_computation.27 | async-start | bytes 8388608
  403.7 14.2 %slice-start.7 = ((s8[17301504]{0:T(1024)(128)(4,1)}), s8[4194304]{0:T(1024)(128)(4,1)S(1)}, s32[]{:S(2)}) async-start(s8[17301504]{0:T(1024)(128)(4,1)} %bitcast.216), calls=%async_computation.28 | async-start | bytes 8388608
  403.7 15.7 %slice-start.8 = ((s8[17301504]{0:T(1024)(128)(4,1)}), s8[4194304]{0:T(1024)(128)(4,1)S(1)}, s32[]{:S(2)}) async-start(s8[17301504]{0:T(1024)(128)(4,1)} %bitcast.216), calls=%async_computation.29 | async-start | bytes 8388608
  403.7 15.7 %slice-start.9 = ((s8[17301504]{0:T(1024)(128)(4,1)}), s8[524288]{0:T(1024)(128)(4,1)S(1)}, s32[]{:S(2)}) async-start(s8[17301504]{0:T(1024)(128)(4,1)} %bitcast.216), calls=%async_computation.30 | async-start | bytes 1048576
  441.5 44.7 %copy-start.3 = (f32[256,1,1024]{2,0,1:T(8,128)S(1)}, f32[256,1,1024]{2,0,1:T(8,128)}, u32[]{:S(2)}) copy-start(f32[256,1,1024]{2,0,1:T(8,128)} %copy-done.2) | copy-start | bytes 3145732
  441.5 44.7 %copy-start.61 = (f32[256]{0:T(256)S(1)}, f32[256]{0:T(256)}, u32[]{:S(2)}) copy-start(f32[256]{0:T(256)} %copy-done.60) | copy-start | bytes 3076
  441.5 46.9 %copy-start.65 = (f32[256]{0:T(256)S(1)}, f32[256]{0:T(256)}, u32[]{:S(2)}) copy-start(f32[256]{0:T(256)} %copy-done.64) | copy-start | bytes 3076
  441.5 50.4 %copy-start.52 = (f32[4,1024]{1,0:T(4,128)S(1)}, f32[4,1024]{1,0:T(4,128)}, u32[]{:S(2)}) copy-start(f32[4,1024]{1,0:T(4,128)} %copy-done.51) | copy-start | bytes 49156
  441.5 50.4 %copy-start.55 = (f32[4,1024]{1,0:T(4,128)S(1)}, f32[4,1024]{1,0:T(4,128)}, u32[]{:S(2)}) copy-start(f32[4,1024]{1,0:T(4,128)} %copy-done.54) | copy-start | bytes 49156
  441.6 73.1 %copy-start.39 = (bf16[256,1024]{1,0:T(8,128)(2,1)S(1)}, bf16[256,1024]{1,0:T(8,128)(2,1)}, u32[]{:S(2)}) copy-start(bf16[256,1024]{1,0:T(8,128)(2,1)} %param.31) | copy-start | bytes 1572868
  441.6 73.1 %all-gather.20.cloned.1.call-start = ((), (), s32[]{:S(2)}) async-start(), calls=%async_computation.17 | async-start | bytes 2621440 | tf_op jit(solution)/shard_map/all_gather | solution.py:298
  490.0 27.0 %copy-start.34 = (bf16[1024,256]{0,1:T(8,128)(2,1)S(1)}, bf16[1024,256]{0,1:T(8,128)(2,1)}, u32[]{:S(2)}) copy-start(bf16[1024,256]{0,1:T(8,128)(2,1)} %copy-done.33) | copy-start | bytes 1572868
  490.0 27.0 %copy-start.46 = (bf16[1,30,256]{1,2,0:T(8,128)(2,1)S(1)}, bf16[1,30,256]{1,2,0:T(8,128)(2,1)}, u32[]{:S(2)}) copy-start(bf16[1,30,256]{1,2,0:T(8,128)(2,1)} %copy-done.45) | copy-start | bytes 46084
  491.9 113.0 %reduce-scatter.17.cloned.1.call-start = ((), (), s32[]{:S(2)}) async-start(), calls=%async_computation.18 | async-start | bytes 2621440 | tf_op jit(solution)/shard_map/reduce_scatter | solution.py:327
  517.0 15.9 %slice-start = ((s8[17301504]{0:T(1024)(128)(4,1)}), s8[4194304]{0:T(1024)(128)(4,1)S(1)}, s32[]{:S(2)}) async-start(s8[17301504]{0:T(1024)(128)(4,1)} %bitcast.214), calls=%async_computation.21 | async-start | bytes 8388608
  517.0 15.8 %slice-start.1 = ((s8[17301504]{0:T(1024)(128)(4,1)}), s8[4194304]{0:T(1024)(128)(4,1)S(1)}, s32[]{:S(2)}) async-start(s8[17301504]{0:T(1024)(128)(4,1)} %bitcast.214), calls=%async_computation.22 | async-start | bytes 8388608
  517.0 15.8 %slice-start.2 = ((s8[17301504]{0:T(1024)(128)(4,1)}), s8[4194304]{0:T(1024)(128)(4,1)S(1)}, s32[]{:S(2)}) async-start(s8[17301504]{0:T(1024)(128)(4,1)} %bitcast.214), calls=%async_computation.23 | async-start | bytes 8388608
  517.0 15.8 %slice-start.3 = ((s8[17301504]{0:T(1024)(128)(4,1)}), s8[4194304]{0:T(1024)(128)(4,1)S(1)}, s32[]{:S(2)}) async-start(s8[17301504]{0:T(1024)(128)(4,1)} %bitcast.214), calls=%async_computation.24 | async-start | bytes 8388608
  517.0 16.2 %slice-start.4 = ((s8[17301504]{0:T(1024)(128)(4,1)}), s8[524288]{0:T(1024)(128)(4,1)S(1)}, s32[]{:S(2)}) async-start(s8[17301504]{0:T(1024)(128)(4,1)} %bitcast.214), calls=%async_computation.25 | async-start | bytes 1048576
  557.3 179.9 %all-reduce.8.cloned.1.call-start = ((), (), s32[]{:S(2)}) async-start(), calls=%async_computation.19 | async-start | bytes 8388608 | tf_op jit(solution)/shard_map/psum | solution.py:346
  559.4 44.4 %slice-start.13 = ((f32[1,1054,4,64]{1,3,2,0:T(8,128)}), f32[1,30,4,64]{1,3,2,0:T(8,128)S(1)}, s32[]{:S(2)}) async-start(f32[1,1054,4,64]{1,3,2,0:T(8,128)} %fusion.22), calls=%async_computation.34 | async-start | bytes 262144 | tf_op jit(solution)/shard_map/slice | solution.py:99
  559.4 44.5 %slice-start.11 = ((f32[1,1054,4,64]{1,3,2,0:T(8,128)}), f32[1,30,4,64]{1,3,2,0:T(8,128)S(1)}, s32[]{:S(2)}) async-start(f32[1,1054,4,64]{1,3,2,0:T(8,128)} %copy-done.17), calls=%async_computation.32 | async-start | bytes 262144 | tf_op jit(solution)/shard_map/slice | solution.py:98
  561.3 43.6 %copy-start.10 = (f32[256,1,1024]{2,0,1:T(8,128)S(1)}, f32[256,1,1024]{2,0,1:T(8,128)}, u32[]{:S(2)}) copy-start(f32[256,1,1024]{2,0,1:T(8,128)} %copy-done.9) | copy-start | bytes 3145732
  561.3 248.1 %all-reduce.10.cloned.1.call-start = ((), (), s32[]{:S(2)}) async-start(), calls=%async_computation.20 | async-start | bytes 245760 | tf_op jit(solution)/shard_map/psum | solution.py:338
  (38 other events, 104.5 us)
Sparse Core Ops, SparseCore 0:
  9.6 25.2 all-gather.7
  69.6 44.4 reduce-scatter.6
  115.7 22.5 all-gather.9
  140.4 22.5 all-gather.11
  194.6 31.4 reduce-scatter.8
  229.7 22.5 all-gather.13
  271.7 31.4 reduce-scatter.10
  309.3 22.5 all-gather.15
  342.7 31.4 reduce-scatter.12
  378.4 22.5 all-gather.17
  441.7 44.4 reduce-scatter.14
  492.0 22.5 all-gather.19
  557.4 31.5 reduce-scatter.16
  595.1 141.9 all-reduce.7
  741.0 68.2 all-reduce.9
where the time goes:
time: 833 us; the launch traced here: 824 us
  waiting for transfers between devices  516 us (62%)
  matrix products  158 us (19%)
  other arithmetic  57.7 us (7%)
  blocking collectives  40.4 us (5%)
  local copies, waits for them, and re-layouts  24.2 us (3%)
  between operations  15.4 us (2%)
  starting transfers between devices  12 us (1%)
    psum x1, waiting for transfers between devices, per_device(): lax.psum((jnp.stack([gain_one, gain_two, gain_three]), jnp.stack([shift_o...  130 us
    dot_general x25, matrix products, product(): return jnp.dot(left_side, right_side, preferred_element_type=jnp.float32)  73.3 us
    psum x1, waiting for transfers between devices, per_device(): lax.psum((self_prefix_part, cross_prefix_part), 'rows')  72.2 us
    reduce_scatter x1, waiting for transfers between devices, per_device(): lax.psum_scatter(jnp.concatenate([to_query, to_memory], axis=1).astype(jn...  44.4 us
    reduce_scatter x1, waiting for transfers between devices, per_device(): lax.psum_scatter(row_terms(self_mixed, self_out, lax.axis_size('tp') * to...  43.5 us
    psum x1, blocking collectives, per_device(): lax.psum((jnp.stack([gain_one, gain_two, gain_three]), jnp.stack([shift_o...  40.4 us
    dot_general x2, matrix products, attend_back(): jnp.einsum('qhd,khd->hqk', grad_heads, value_rows, preferred_element_type...  30 us
    reduce_scatter x1, waiting for transfers between devices, per_device(): lax.psum_scatter(row_terms(hidden.reshape(seq_len, rows_local, -1), ffn_o...  27.6 us
  transfers between devices with their start and end apart: 15, of which 14 were waited for; matrix products, arithmetic and copies ran while one was open for 4% of the time, Pallas kernels for 0%

commit v1 on v0

v1 whole, which is shorter than its diff:
```python
import functools

import jax
import jax.numpy as jnp
from jax import lax
from jax.experimental import pallas as pl
from jax.experimental.pallas import tpu as pltpu
from jax.sharding import PartitionSpec as P

HEAD = 64
PAIR = 2 * HEAD
PRE = 128
PRE_PACK = 32
GROUP = 8
LINE = 4
MASKED = -1000000000.0
EPSILON = 1e-05
SCALE = HEAD**-0.5
f32 = jnp.float32
bf16 = jnp.bfloat16
MESH = pl.DeviceIdType.MESH
VMEM = pltpu.VMEM
ANY = pl.ANY


def nn(a, b):
    return lax.dot_general(a, b, (((1,), (0,)), ((), ())), preferred_element_type=f32)


def nt(a, b):
    return lax.dot_general(a, b, (((1,), (1,)), ((), ())), preferred_element_type=f32)


def tn(a, b):
    return lax.dot_general(a, b, (((0,), (0,)), ((), ())), preferred_element_type=f32)


def gelu_parts(v):
    phi = 0.5 + 0.5 * lax.erf(v * (0.5**0.5))
    slope = phi + v * (jnp.exp(-0.5 * v * v) * 0.3989422804014327)
    return v * phi, slope


def norm_parts(v):
    centered = v - jnp.mean(v, axis=-1, keepdims=True)
    spread = lax.rsqrt(jnp.mean(centered * centered, axis=-1, keepdims=True) + EPSILON)
    return centered * spread, spread


def norm_back(dy, gain, n, spread):
    dn = dy * gain
    dv = spread * (
        dn - jnp.mean(dn, axis=-1, keepdims=True) - n * jnp.mean(dn * n, axis=-1, keepdims=True)
    )
    return dv, jnp.sum(dy * n, axis=0, keepdims=True), jnp.sum(dy, axis=0, keepdims=True)


def lane_half(shape, h):
    return (lax.broadcasted_iota(jnp.int32, shape, 1) // HEAD) == h


def mask_bias(seg_q, seg_k, q_index, k_index, prefix_len):
    keep = seg_q == seg_k
    if q_index is not None:
        keep = keep & (k_index - PRE <= q_index)
    keep = keep | (k_index < prefix_len)
    return jnp.where(keep, 0.0, MASKED)


def pair_forward(q_pair, k_pair, v_pair, bias):
    outs = []
    for h in range(2):
        half = lane_half(q_pair.shape, h)
        scores = nt(jnp.where(half, q_pair, jnp.zeros_like(q_pair)), k_pair) + bias
        top = jnp.max(scores, axis=1, keepdims=True)
        e = jnp.exp(scores - top)
        total = jnp.sum(e, axis=1, keepdims=True)
        outs.append(nn(e.astype(bf16), v_pair) * (1.0 / total))
    return jnp.where(lane_half(outs[0].shape, 0), outs[0], outs[1]).astype(bf16)


def pair_backward(q_pair, k_pair, v_pair, da_pair, bias_t):
    k_turned = k_pair.T
    dk = dv = None
    dq = []
    for h in range(2):
        half = lane_half(q_pair.shape, h)
        q = jnp.where(half, q_pair, jnp.zeros_like(q_pair))
        da = jnp.where(half, da_pair, jnp.zeros_like(da_pair))
        scores = nt(k_pair, q) + bias_t
        top = jnp.max(scores, axis=0, keepdims=True)
        e = jnp.exp(scores - top)
        p = e * (1.0 / jnp.sum(e, axis=0, keepdims=True))
        weighted = p * nt(v_pair, da)
        ds = (weighted - p * jnp.sum(weighted, axis=0, keepdims=True)).astype(bf16)
        dv_h = nn(p.astype(bf16), da)
        dk_h = nn(ds, q)
        dk = dk_h if dk is None else dk + dk_h
        dv = dv_h if dv is None else dv + dv_h
        dq.append(nn(k_turned[h * HEAD : (h + 1) * HEAD], ds))
    return jnp.concatenate(dq, axis=0).T.astype(bf16), dk, dv


def self_forward_kernel(
    prefix_len, x, wq, wk, wv, wo, pre, seg_col, seg_row, q_out, k_out, v_out, part, mixed, bias
):
    block = q_out.shape[0] // 4
    lanes = q_out.shape[1]
    for target, at in ((k_out, 0), (v_out, PRE_PACK)):
        target[0:PRE_PACK] = pre[at : at + PRE_PACK]
        target[PRE_PACK:PRE] = jnp.zeros((PRE - PRE_PACK, lanes), bf16)

    @pl.loop(0, 4)
    def _(i):
        at = pl.multiple_of(i * block, block)
        rows = x[pl.ds(at, block)]
        q_out[pl.ds(at, block)] = (SCALE * nn(rows, wq[...])).astype(bf16)
        k_out[pl.ds(PRE + at, block)] = nn(rows, wk[...]).astype(bf16)
        v_out[pl.ds(PRE + at, block)] = nn(rows, wv[...]).astype(bf16)

    for i in range(4):
        keys = PRE + (i + 1) * block
        shape = (block, keys)
        bias[:, 0:keys] = mask_bias(
            seg_col[i * block : (i + 1) * block],
            seg_row[:, 0:keys],
            i * block + lax.broadcasted_iota(jnp.int32, shape, 0),
            lax.broadcasted_iota(jnp.int32, shape, 1),
            prefix_len,
        )

        @pl.loop(0, lanes // PAIR)
        def _(j):
            cols = pl.ds(pl.multiple_of(j * PAIR, PAIR), PAIR)
            mixed[:, cols] = pair_forward(
                q_out[i * block : (i + 1) * block, cols],
                k_out[0:keys, cols],
                v_out[0:keys, cols],
                bias[:, 0:keys],
            )

        part[i] = nn(mixed[...], wo[...]).astype(bf16)


def self_forward(prefix_len, x_full, wq, wk, wv, wo, pre, seg_col, seg_row):
    n, seq_local, width = x_full.shape
    seq, lanes = n * seq_local, wq.shape[1]
    out = jax.ShapeDtypeStruct
    return pl.pallas_call(
        functools.partial(self_forward_kernel, prefix_len),
        out_shape=(
            out((seq, lanes), bf16),
            out((PRE + seq, lanes), bf16),
            out((PRE + seq, lanes), bf16),
            out((n, seq_local, width), bf16),
        ),
        in_specs=[pl.BlockSpec(memory_space=VMEM)] * 8,
        out_specs=[pl.BlockSpec(memory_space=VMEM)] * 4,
        scratch_shapes=[
            VMEM((seq_local, lanes), bf16),
            VMEM((seq_local, PRE + seq), f32),
        ],
        compiler_params=pltpu.CompilerParams(vmem_limit_bytes=48 << 20),
        name="self_forward",
    )(x_full.reshape(seq, width), wq, wk, wv, wo, pre, seg_col, seg_row)


def cross_forward_kernel(
    prefix_len, v1, memory, wq, wk, wv, wo, pre, seg_col, seg_row, gain, shift,
    q_out, k_out, v_out, v2, n1_low, bias, mixed,
):
    step = pl.program_id(0)
    block, lanes = q_out.shape[1:]
    keys = k_out.shape[1]

    @pl.when(step == 0)
    def _():
        n, _ = norm_parts(v1[...])
        normed = n * gain[0:1] + shift[0:1]
        v2[...] = normed
        n1_low[...] = normed.astype(bf16)
        bias[...] = mask_bias(
            seg_col[...],
            seg_row[...],
            None,
            lax.broadcasted_iota(jnp.int32, (block, keys), 1),
            prefix_len,
        )

    q_out[0] = (SCALE * nn(n1_low[...], wq[0])).astype(bf16)
    for target, at in ((k_out, 0), (v_out, PRE_PACK)):
        target[0, 0:PRE_PACK] = pre[0, at : at + PRE_PACK]
        target[0, PRE_PACK:PRE] = jnp.zeros((PRE - PRE_PACK, lanes), bf16)

    @pl.loop(0, (keys - PRE) // block)
    def _(i):
        at = pl.multiple_of(i * block, block)
        rows = memory[pl.ds(at, block)]
        k_out[0, pl.ds(PRE + at, block)] = nn(rows, wk[0]).astype(bf16)
        v_out[0, pl.ds(PRE + at, block)] = nn(rows, wv[0]).astype(bf16)

    @pl.loop(0, lanes // PAIR)
    def _(j):
        cols = pl.ds(pl.multiple_of(j * PAIR, PAIR), PAIR)
        mixed[:, cols] = pair_forward(
            q_out[0, :, cols], k_out[0, :, cols], v_out[0, :, cols], bias[...]
        )

    v2[...] += nn(mixed[...], wo[0])


def whole_spec(shape):
    return pl.BlockSpec(shape, lambda i: (0,) * len(shape))


def shard_spec(shape, index=lambda i: i):
    return pl.BlockSpec((1,) + shape[1:], lambda i: (index(i), 0, 0))


def cross_forward(prefix_len, v1, memory, weights, pre, seg_col, seg_row, gain, shift):
    wq, wk, wv, wo = weights
    n, width, lanes = wq.shape
    block = v1.shape[0]
    seq = memory.shape[0]
    out = jax.ShapeDtypeStruct
    outs = (
        out((n, block, lanes), bf16),
        out((n, PRE + seq, lanes), bf16),
        out((n, PRE + seq, lanes), bf16),
    )
    return pl.pallas_call(
        functools.partial(cross_forward_kernel, prefix_len),
        grid=(n,),
        out_shape=outs + (out((block, width), f32),),
        in_specs=[whole_spec(v1.shape), whole_spec(memory.shape)]
        + [shard_spec(a.shape) for a in (wq, wk, wv, wo, pre)]
        + [whole_spec(a.shape) for a in (seg_col, seg_row, gain, shift)],
        out_specs=[shard_spec(a.shape) for a in outs] + [whole_spec((block, width))],
        scratch_shapes=[
            VMEM((block, width), bf16),
            VMEM((block, PRE + seq), f32),
            VMEM((block, lanes), bf16),
        ],
        compiler_params=pltpu.CompilerParams(vmem_limit_bytes=48 << 20),
        name="cross_forward",
    )(v1, memory, wq, wk, wv, wo, pre, seg_col, seg_row, gain, shift)


def feed_forward_kernel(
    v2, out_grad, w_in, w_out, down, down_bias, up, up_bias, gain, shift,
    output, dr2, up_grad, down_grad, vecs,
    n2_low, n2_hat, total, e_low, slope, grad,
):
    step = pl.program_id(0)
    half = pl.num_programs(0) // 2
    width = v2.shape[1]

    @pl.when(step == 0)
    def _():
        n, _ = norm_parts(v2[...])
        n2_hat[...] = n
        normed = n * gain[1:2] + shift[1:2]
        total[...] = normed
        n2_low[...] = normed.astype(bf16)

    @pl.when(step < half)
    def _():
        act, bend = gelu_parts(nn(n2_low[...], w_in[0]))
        slope[step] = bend
        total[...] += nn(act.astype(bf16), w_out[0])

    @pl.when(step == half - 1)
    def _():
        act, bend = gelu_parts(nn(n2_low[...], down[...]) + down_bias[...])
        act = act.astype(bf16)
        resid = total[...] + 4.0 * (nn(act, up[...]) + up_bias[...])
        n, spread = norm_parts(resid)
        output[...] = (n * gain[2:3] + shift[2:3]).astype(bf16)
        dz, gain_part, shift_part = norm_back(out_grad[...].astype(f32), gain[2:3], n, spread)
        e_low[...] = dz.astype(bf16)
        four = (4.0 * dz).astype(bf16)
        up_grad[...] = tn(act, four).astype(bf16)
        da = (nt(four, up[...]) * bend).astype(bf16)
        down_grad[...] = tn(da, n2_low[...]).astype(bf16)
        grad[...] = dz + nt(da, down[...])
        vecs[...] = jnp.zeros_like(vecs)
        vecs[2:3] = gain_part
        vecs[5:6] = shift_part
        vecs[6:7] = jnp.sum(four.astype(f32), axis=0, keepdims=True)
        vecs[7:8, 0 : down.shape[1]] = jnp.sum(da.astype(f32), axis=0, keepdims=True)

    @pl.when(step >= half)
    def _():
        du = (nt(e_low[...], w_out[0]) * slope[2 * half - 1 - step]).astype(bf16)
        grad[...] += nt(du, w_in[0])

    @pl.when(step == 2 * half - 1)
    def _():
        _, spread = norm_parts(v2[...])
        dv, gain_part, shift_part = norm_back(grad[...], gain[1:2], n2_hat[...], spread)
        dr2[...] = dv
        vecs[1:2] = gain_part
        vecs[4:5] = shift_part


def feed_forward(v2, out_grad, w_in, w_out, down, down_bias, up, up_bias, gain, shift):
    n, width, inner = w_in.shape
    block = v2.shape[0]
    adapt = down.shape[1]
    out = jax.ShapeDtypeStruct
    outs = (
        out((block, width), bf16),
        out((block, width), f32),
        out((adapt, width), bf16),
        out((adapt, width), bf16),
        out((8, width), f32),
    )
    turn = lambda i: jnp.minimum(i, 2 * n - 1 - i)
    return pl.pallas_call(
        feed_forward_kernel,
        grid=(2 * n,),
        out_shape=outs,
        in_specs=[whole_spec(v2.shape), whole_spec(out_grad.shape)]
        + [shard_spec(w_in.shape, turn), shard_spec(w_out.shape, turn)]
        + [whole_spec(a.shape) for a in (down, down_bias, up, up_bias, gain, shift)],
        out_specs=[whole_spec(a.shape) for a in outs],
        scratch_shapes=[
            VMEM((block, width), bf16),
            VMEM((block, width), f32),
            VMEM((block, width), f32),
            VMEM((block, width), bf16),
            VMEM((n, block, inner), f32),
            VMEM((block, width), f32),
        ],
        compiler_params=pltpu.CompilerParams(vmem_limit_bytes=56 << 20),
        name="feed_forward",
    )(v2, out_grad, w_in, w_out, down, down_bias, up, up_bias, gain, shift)


def cross_backward_kernel(
    prefix_len, dr2, v1, q, k, v, wq, wk, wv, wo, seg_row, seg_col, gain,
    dr1, dr1_low, dm_out, pre_grad, vecs,
    dr2_low, bias, da, dq, dk, dv, total, dm,
):
    step = pl.program_id(0)
    steps = pl.num_programs(0)
    block, lanes = q.shape[1:]
    keys = k.shape[1]

    @pl.when(step == 0)
    def _():
        dr2_low[...] = dr2[...].astype(bf16)
        total[...] = jnp.zeros_like(total)
        dm[...] = jnp.zeros_like(dm)
        bias[...] = mask_bias(
            seg_row[...],
            seg_col[...],
            None,
            lax.broadcasted_iota(jnp.int32, (keys, block), 0),
            prefix_len,
        )

    da[...] = nt(dr2_low[...], wo[0]).astype(bf16)

    @pl.loop(0, lanes // PAIR)
    def _(j):
        cols = pl.ds(pl.multiple_of(j * PAIR, PAIR), PAIR)
        dq_pair, dk_pair, dv_pair = pair_backward(
            q[0, :, cols], k[0, :, cols], v[0, :, cols], da[:, cols], bias[...]
        )
        dq[:, cols] = dq_pair
        pre_grad[0, 0:PRE_PACK, cols] = dk_pair[0:PRE_PACK]
        pre_grad[0, PRE_PACK : 2 * PRE_PACK, cols] = dv_pair[0:PRE_PACK]
        dk[:, cols] = dk_pair[PRE:].astype(bf16)
        dv[:, cols] = dv_pair[PRE:].astype(bf16)

    total[...] += nt(dq[...], wq[0])

    @pl.loop(0, (keys - PRE) // block)
    def _(i):
        rows = pl.ds(pl.multiple_of(i * block, block), block)
        dm[rows] += nt(dk[rows], wk[0]) + nt(dv[rows], wv[0])

    @pl.when(step == steps - 1)
    def _():
        n, spread = norm_parts(v1[...])
        grad, gain_part, shift_part = norm_back(
            dr2[...] + SCALE * total[...], gain[0:1], n, spread
        )
        dr1[...] = grad
        dr1_low[...] = grad.astype(bf16)
        vecs[...] = jnp.zeros_like(vecs)
        vecs[0:1] = gain_part
        vecs[3:4] = shift_part

        @pl.loop(0, (keys - PRE) // block)
        def _(i):
            rows = pl.ds(pl.multiple_of(i * block, block), block)
            dm_out[rows] = dm[rows].astype(bf16)


def cross_backward(prefix_len, dr2, v1, q, k, v, weights, seg_row, seg_col, gain):
    wq, wk, wv, wo = weights
    n, block, lanes = q.shape
    keys = k.shape[1]
    width = dr2.shape[1]
    out = jax.ShapeDtypeStruct
    outs = (
        out((block, width), f32),
        out((block, width), bf16),
        out((keys - PRE, width), bf16),
        out((n, 2 * PRE_PACK, lanes), f32),
        out((8, width), f32),
    )
    out_specs = [whole_spec(a.shape) for a in outs]
    out_specs[3] = shard_spec(outs[3].shape)
    return pl.pallas_call(
        functools.partial(cross_backward_kernel, prefix_len),
        grid=(n,),
        out_shape=outs,
        in_specs=[whole_spec(dr2.shape), whole_spec(v1.shape)]
        + [shard_spec(a.shape) for a in (q, k, v, wq, wk, wv, wo)]
        + [whole_spec(a.shape) for a in (seg_row, seg_col, gain)],
        out_specs=out_specs,
        scratch_shapes=[
            VMEM((block, width), bf16),
            VMEM((keys, block), f32),
            VMEM((block, lanes), bf16),
            VMEM((block, lanes), bf16),
            VMEM((keys - PRE, lanes), bf16),
            VMEM((keys - PRE, lanes), bf16),
            VMEM((block, width), f32),
            VMEM((keys - PRE, width), f32),
        ],
        compiler_params=pltpu.CompilerParams(vmem_limit_bytes=56 << 20),
        name="cross_backward",
    )(dr2, v1, q, k, v, wq, wk, wv, wo, seg_row, seg_col, gain)


def self_backward_kernel(
    prefix_len, dr1, q, k, v, wq, wk, wv, wo, seg_row, seg_col,
    part, pre_grad, bias, da, dq, dk, dv,
):
    seq, lanes = q.shape
    block = seq // 4
    dk[...] = jnp.zeros_like(dk)
    dv[...] = jnp.zeros_like(dv)

    for i in reversed(range(4)):
        rows = slice(i * block, (i + 1) * block)
        keys = PRE + (i + 1) * block
        shape = (keys, block)
        bias[0:keys] = mask_bias(
            seg_row[:, rows],
            seg_col[0:keys],
            i * block + lax.broadcasted_iota(jnp.int32, shape, 1),
            lax.broadcasted_iota(jnp.int32, shape, 0),
            prefix_len,
        )
        da[...] = nt(dr1[i], wo[...]).astype(bf16)

        @pl.loop(0, lanes // PAIR)
        def _(j):
            cols = pl.ds(pl.multiple_of(j * PAIR, PAIR), PAIR)
            dq_pair, dk_pair, dv_pair = pair_backward(
                q[rows, cols], k[0:keys, cols], v[0:keys, cols], da[:, cols], bias[0:keys]
            )
            dq[:, cols] = dq_pair
            dk[0:keys, cols] += dk_pair
            dv[0:keys, cols] += dv_pair

        done = slice(PRE + i * block, PRE + (i + 1) * block)
        part[i] = (
            SCALE * nt(dq[...], wq[...])
            + nt(dk[done].astype(bf16), wk[...])
            + nt(dv[done].astype(bf16), wv[...])
        ).astype(bf16)

    pre_grad[0:PRE_PACK] = dk[0:PRE_PACK]
    pre_grad[PRE_PACK : 2 * PRE_PACK] = dv[0:PRE_PACK]


def self_backward(prefix_len, dr1_full, q, k, v, wq, wk, wv, wo, seg_row, seg_col):
    n, block, width = dr1_full.shape
    seq, lanes = q.shape
    out = jax.ShapeDtypeStruct
    return pl.pallas_call(
        functools.partial(self_backward_kernel, prefix_len),
        out_shape=(out((n, block, width), bf16), out((2 * PRE_PACK, lanes), f32)),
        in_specs=[pl.BlockSpec(memory_space=VMEM)] * 10,
        out_specs=[pl.BlockSpec(memory_space=VMEM)] * 2,
        scratch_shapes=[
            VMEM((PRE + seq, block), f32),
            VMEM((block, lanes), bf16),
            VMEM((block, lanes), bf16),
            VMEM((PRE + seq, lanes), f32),
            VMEM((PRE + seq, lanes), f32),
        ],
        compiler_params=pltpu.CompilerParams(vmem_limit_bytes=48 << 20),
        name="self_backward",
    )(dr1_full, q, k, v, wq, wk, wv, wo, seg_row, seg_col)


class Links:
    def __init__(self, send, recv):
        self.send, self.recv = send, recv
        self.row = lax.axis_index("rows")
        self.t = lax.axis_index("tp")
        self.flows = 0
        place = lax.rem(self.row, GROUP)
        self.base = self.row - place
        self.a = place // 2
        self.b = lax.rem(place, 2)
        self.place = place

    def flow(self):
        self.flows += 1
        return self.flows - 1

    def tp_peer(self, mask):
        return (self.row, self.t ^ mask)

    def line_peer(self, d):
        return (self.base + lax.rem(self.a + d, LINE) * 2 + self.b, self.t)

    def side_peer(self):
        return (self.base + self.a * 2 + (1 - self.b), self.t)

    def copy(self, src, dst, flow, peer):
        return pltpu.make_async_remote_copy(
            src_ref=src,
            dst_ref=dst,
            send_sem=self.send.at[flow],
            recv_sem=self.recv.at[flow],
            device_id=peer,
            device_id_type=MESH,
        )

    def start(self, src, dst, flow, peer):
        made = self.copy(src, dst, flow, peer)
        made.start()
        return made

    def arrived(self, dst, flow, peer):
        self.copy(dst, dst, flow, peer).wait_recv()


def greet(peers):
    barrier = pltpu.get_barrier_semaphore()
    for peer in peers:
        pl.semaphore_signal(barrier, inc=1, device_id=peer, device_id_type=MESH)
    pl.semaphore_wait(barrier, len(peers))


CHUNKS = 4


def gather_rows_start(links, own, full):
    rows = own.shape[0] // CHUNKS
    t = links.t
    flow = links.flow()
    sends = [links.start(own, full.at[t], flow, links.tp_peer(1))]
    chunk_flows = []
    for c in range(CHUNKS):
        at = pl.ds(c * rows, rows)
        f = links.flow()
        chunk_flows.append(f)
        sends.append(links.start(own.at[at], full.at[t, at], f, links.tp_peer(2)))
    return flow, chunk_flows, sends


def gather_rows_pass(links, full, state):
    flow, chunk_flows, sends = state
    rows = full.shape[1] // CHUNKS
    far, beside, last = links.t ^ 2, links.t ^ 1, links.t ^ 3
    passed = []
    for c in range(CHUNKS):
        at = pl.ds(c * rows, rows)
        links.arrived(full.at[far, at], chunk_flows[c], links.tp_peer(2))
        f = links.flow()
        passed.append(f)
        sends.append(links.start(full.at[far, at], full.at[far, at], f, links.tp_peer(1)))
    links.arrived(full.at[beside], flow, links.tp_peer(1))
    for c in range(CHUNKS):
        at = pl.ds(c * rows, rows)
        links.arrived(full.at[last, at], passed[c], links.tp_peer(1))
    return sends


def gather_kernel(count, *refs):
    own, full = refs[:count], refs[count : 2 * count]
    send, recv, local = refs[2 * count :]
    links = Links(send, recv)
    greet([links.tp_peer(1), links.tp_peer(2)])
    kept = [pltpu.make_async_copy(own[i], full[i].at[links.t], local.at[i]) for i in range(count)]
    for one in kept:
        one.start()
    states = [gather_rows_start(links, own[i], full[i]) for i in range(count)]
    for i in range(count):
        for one in gather_rows_pass(links, full[i], states[i]):
            one.wait_send()
    for one in kept:
        one.wait()


def gather_rows(collective_id, *own):
    n = 4
    flows = (1 + 2 * CHUNKS) * len(own)
    return pl.pallas_call(
        functools.partial(gather_kernel, len(own)),
        out_shape=tuple(jax.ShapeDtypeStruct((n,) + a.shape, a.dtype) for a in own),
        in_specs=[pl.BlockSpec(memory_space=ANY)] * len(own),
        out_specs=[pl.BlockSpec(memory_space=ANY)] * len(own),
        scratch_shapes=[
            pltpu.SemaphoreType.DMA((flows,)),
            pltpu.SemaphoreType.DMA((flows,)),
            pltpu.SemaphoreType.DMA((len(own),)),
        ],
        compiler_params=pltpu.CompilerParams(
            collective_id=collective_id, has_side_effects=True
        ),
        name="gather_rows",
    )(*own)


def gather_all_kernel(count, *refs):
    x, memory, pre = refs[0:3]
    own = refs[3 : 3 + count]
    x_full, m_full, pre_full = refs[3 + count : 6 + count]
    full = refs[6 + count : 6 + 2 * count]
    send, recv, local = refs[6 + 2 * count :]
    links = Links(send, recv)
    t, far, last = links.t, links.t ^ 2, links.t ^ 3
    greet(
        [links.tp_peer(m) for m in (1, 2, 3)]
        + [links.line_peer(d) for d in range(1, LINE)]
        + [links.side_peer()]
    )
    kept = []
    for i, (src, dst) in enumerate(
        [(x, x_full), (memory, m_full), (pre, pre_full)] + list(zip(own, full))
    ):
        kept.append(pltpu.make_async_copy(src, dst.at[t], local.at[i]))
        kept[-1].start()
    sends = []
    state = gather_rows_start(links, x, x_full)
    pre_flows = []
    for m in (1, 2, 3):
        pre_flows.append(links.flow())
        sends.append(links.start(pre, pre_full.at[t], pre_flows[-1], links.tp_peer(m)))
    beside = []
    across = []
    for i in range(count):
        rows = own[i].shape[0] // GROUP
        at = pl.ds(pl.multiple_of(links.place * rows, rows), rows)
        across.append(links.flow())
        sends.append(links.start(own[i].at[at], full[i].at[t, at], across[-1], links.tp_peer(2)))
        beside.append(links.flow())
        sends.append(links.start(own[i], full[i].at[t], beside[-1], links.tp_peer(1)))
    state_m = gather_rows_start(links, memory, m_full)
    line_flows, side_flows = [], []
    for i in range(count):
        rows = own[i].shape[0] // GROUP
        mine = full[i].at[far, pl.ds(pl.multiple_of(links.place * rows, rows), rows)]
        links.arrived(mine, across[i], links.tp_peer(2))
        flows = []
        for d in range(1, LINE):
            flows.append(links.flow())
            sends.append(links.start(mine, mine, flows[-1], links.line_peer(d)))
        line_flows.append(flows)
        side_flows.append([links.flow()])
        sends.append(links.start(mine, mine, side_flows[i][0], links.side_peer()))
    sends += gather_rows_pass(links, x_full, state)
    for i in range(count):
        rows = own[i].shape[0] // GROUP
        for d in range(1, LINE):
            piece = lax.rem(links.a - d + LINE, LINE) * 2 + links.b
            here = full[i].at[far, pl.ds(pl.multiple_of(piece * rows, rows), rows)]
            links.arrived(here, line_flows[i][d - 1], links.line_peer(d))
            side_flows[i].append(links.flow())
            sends.append(links.start(here, here, side_flows[i][d], links.side_peer()))
    sends += gather_rows_pass(links, m_full, state_m)
    passed = []
    for i in range(count):
        rows = own[i].shape[0] // GROUP
        for d in range(LINE):
            piece = lax.rem(links.a - d + LINE, LINE) * 2 + (1 - links.b)
            here = full[i].at[far, pl.ds(pl.multiple_of(piece * rows, rows), rows)]
            links.arrived(here, side_flows[i][d], links.side_peer())
        passed.append(links.flow())
        sends.append(links.start(full[i].at[far], full[i].at[far], passed[i], links.tp_peer(1)))
    for m in (1, 2, 3):
        links.arrived(pre_full.at[t ^ m], pre_flows[m - 1], links.tp_peer(m))
    for i in range(count):
        links.arrived(full[i].at[t ^ 1], beside[i], links.tp_peer(1))
        links.arrived(full[i].at[last], passed[i], links.tp_peer(1))
    for one in sends:
        one.wait_send()
    for one in kept:
        one.wait()


def gather_all(collective_id, x, memory, pre, weights):
    n = 4
    count = len(weights)
    given = (x, memory, pre) + tuple(weights)
    flows = 2 * (1 + 2 * CHUNKS) + 3 + count * (3 + 2 * LINE - 1)
    return pl.pallas_call(
        functools.partial(gather_all_kernel, count),
        out_shape=tuple(jax.ShapeDtypeStruct((n,) + a.shape, a.dtype) for a in given),
        in_specs=[pl.BlockSpec(memory_space=ANY)] * len(given),
        out_specs=[pl.BlockSpec(memory_space=ANY)] * len(given),
        scratch_shapes=[
            pltpu.SemaphoreType.DMA((flows,)),
            pltpu.SemaphoreType.DMA((flows,)),
            pltpu.SemaphoreType.DMA((len(given),)),
        ],
        compiler_params=pltpu.CompilerParams(
            collective_id=collective_id, has_side_effects=True
        ),
        name="gather_all",
    )(*given)


def scatter_kernel(count, bases, *refs):
    parts = refs[:count]
    base = refs[count : count + bases]
    outs = refs[count + bases : 2 * count + bases]
    near, near_far, mid, far = refs[2 * count + bases : 2 * count + bases + 4]
    send, recv = refs[2 * count + bases + 4 :]
    links = Links(send, recv)
    t = links.t
    greet([links.tp_peer(1), links.tp_peer(2)])
    rows = parts[0].shape[1] // CHUNKS
    sends, first, second, across = [], [], [], []
    for i in range(count):
        first.append(links.flow())
        sends.append(
            links.start(parts[i].at[t ^ 3], near_far.at[i], first[i], links.tp_peer(1))
        )
        second.append(links.flow())
        sends.append(links.start(parts[i].at[t ^ 1], near.at[i], second[i], links.tp_peer(1)))
    for i in range(count):
        links.arrived(near_far.at[i], first[i], links.tp_peer(1))
        across.append([])
        for c in range(CHUNKS):
            at = pl.ds(c * rows, rows)
            mid[i, at] = (
                parts[i][t ^ 2, at].astype(f32) + near_far[i, at].astype(f32)
            ).astype(bf16)
            across[i].append(links.flow())
            sends.append(
                links.start(mid.at[i, at], far.at[i, at], across[i][c], links.tp_peer(2))
            )
    for i in range(count):
        links.arrived(near.at[i], second[i], links.tp_peer(1))
        for c in range(CHUNKS):
            at = pl.ds(c * rows, rows)
            links.arrived(far.at[i, at], across[i][c], links.tp_peer(2))
            value = (
                parts[i][t, at].astype(f32)
                + near[i, at].astype(f32)
                + far[i, at].astype(f32)
            )
            if i < bases:
                value = value + base[i][at].astype(f32)
            outs[i][at] = value.astype(outs[i].dtype)
    for one in sends:
        one.wait_send()


def scatter_sum(collective_id, parts, base, kinds):
    count = len(parts)
    _, block, width = parts[0].shape
    flows = count * (2 + CHUNKS)
    slots = VMEM((count, block, width), bf16)
    return pl.pallas_call(
        functools.partial(scatter_kernel, count, len(base)),
        out_shape=tuple(jax.ShapeDtypeStruct((block, width), kind) for kind in kinds),
        in_specs=[pl.BlockSpec(memory_space=VMEM)] * (count + len(base)),
        out_specs=[pl.BlockSpec(memory_space=VMEM)] * count,
        scratch_shapes=[
            slots,
            slots,
            slots,
            slots,
            pltpu.SemaphoreType.DMA((flows,)),
            pltpu.SemaphoreType.DMA((flows,)),
        ],
        compiler_params=pltpu.CompilerParams(
            collective_id=collective_id, has_side_effects=True, vmem_limit_bytes=40 << 20
        ),
        name="scatter_sum",
    )(*parts, *base)


def adapter_sum_kernel(levels, g, out, s1, h, xb, h2, zb, p3, yb, hb, send, recv):
    links = Links(send, recv)
    t, a, b = links.t, links.a, links.b
    c = lax.rem(t, 2)
    far_groups = []
    for level in range(levels):
        bit = GROUP << level
        far_groups.append((links.row ^ bit, t))
    greet(
        [links.tp_peer(1), links.tp_peer(2)]
        + [links.line_peer(d) for d in range(1, LINE)]
        + [links.side_peer()]
        + far_groups
    )
    sends = []

    def send_to(src, dst, peer):
        flow = links.flow()
        sends.append(links.start(src, dst, flow, peer))
        return flow

    flow = send_to(g.at[1 - c], s1, links.tp_peer(1))
    links.arrived(s1, flow, links.tp_peer(1))
    h[...] = (g[c].astype(f32) + s1[...].astype(f32)).astype(bf16)
    flow = send_to(h.at[1 - b], xb, links.side_peer())
    links.arrived(xb, flow, links.side_peer())
    h2[...] = (h[b].astype(f32) + xb[...].astype(f32)).astype(bf16)
    line = []
    for d in range(1, LINE):
        line.append(send_to(h2.at[lax.rem(a + d, LINE)], zb.at[d - 1], links.line_peer(d)))
    for d in range(1, LINE):
        links.arrived(zb.at[d - 1], line[d - 1], links.line_peer(d))
    total = h2[a].astype(f32)
    for d in range(1, LINE):
        total = total + zb[d - 1].astype(f32)
    p3[...] = total.astype(bf16)
    flow = send_to(p3, yb, links.tp_peer(2))
    links.arrived(yb, flow, links.tp_peer(2))
    value = p3[...].astype(f32) + yb[...].astype(f32)
    for level in range(levels):
        hb[2 * level] = value.astype(bf16)
        flow = send_to(hb.at[2 * level], hb.at[2 * level + 1], far_groups[level])
        links.arrived(hb.at[2 * level + 1], flow, far_groups[level])
        value = hb[2 * level].astype(f32) + hb[2 * level + 1].astype(f32)
    out[c, b, a] = value.astype(bf16)
    mine = out.at[c, b, a]
    line = []
    for d in range(1, LINE):
        line.append(send_to(mine, mine, links.line_peer(d)))
    side = [send_to(mine, mine, links.side_peer())]
    for d in range(1, LINE):
        here = out.at[c, b, lax.rem(a - d + LINE, LINE)]
        links.arrived(here, line[d - 1], links.line_peer(d))
        side.append(send_to(here, here, links.side_peer()))
    for d in range(LINE):
        links.arrived(out.at[c, 1 - b, lax.rem(a - d + LINE, LINE)], side[d], links.side_peer())
    flow = send_to(out.at[c], out.at[c], links.tp_peer(1))
    links.arrived(out.at[1 - c], flow, links.tp_peer(1))
    for one in sends:
        one.wait_send()


def doublings(count):
    levels = 0
    while (1 << levels) < count:
        levels += 1
    return levels


def adapter_sum(collective_id, row_count, grads):
    levels = doublings(row_count // GROUP)
    height, width = grads.shape
    piece = height // (2 * GROUP)
    half = (2, LINE, piece, width)
    flows = 1 + 1 + 3 + 1 + levels + 3 + 4 + 1
    return pl.pallas_call(
        functools.partial(adapter_sum_kernel, levels),
        out_shape=jax.ShapeDtypeStruct((2,) + half, bf16),
        in_specs=[pl.BlockSpec(memory_space=VMEM)],
        out_specs=pl.BlockSpec(memory_space=VMEM),
        scratch_shapes=[
            VMEM(half, bf16),
            VMEM(half, bf16),
            VMEM(half[1:], bf16),
            VMEM(half[1:], bf16),
            VMEM((LINE - 1, piece, width), bf16),
            VMEM((piece, width), bf16),
            VMEM((piece, width), bf16),
            VMEM((max(1, 2 * levels), piece, width), bf16),
            pltpu.SemaphoreType.DMA((flows,)),
            pltpu.SemaphoreType.DMA((flows,)),
        ],
        compiler_params=pltpu.CompilerParams(
            collective_id=collective_id, has_side_effects=True, vmem_limit_bytes=40 << 20
        ),
        name="adapter_sum",
    )(grads.reshape((2,) + half)).reshape(height, width)


def small_sum_kernel(levels, cross, own, vecs, out, cross_in, vecs_in, outgo, income, send, recv):
    links = Links(send, recv)
    t = links.t
    row_peers = [(links.row ^ (1 << level), t) for level in range(levels)]
    greet([links.tp_peer(m) for m in (1, 2, 3)] + row_peers)
    sends = []
    flows = []
    for m in (1, 2, 3):
        peer = links.tp_peer(m)
        for src, dst in ((cross.at[t ^ m], cross_in.at[t]), (vecs, vecs_in.at[t])):
            flow = links.flow()
            flows.append(flow)
            sends.append(links.start(src, dst, flow, peer))
    cross_in[t] = cross[t]
    vecs_in[t] = vecs[...]
    for m in (1, 2, 3):
        links.arrived(cross_in.at[t ^ m], flows[2 * (m - 1)], links.tp_peer(m))
        links.arrived(vecs_in.at[t ^ m], flows[2 * (m - 1) + 1], links.tp_peer(m))
    kept = cross.shape[1]
    height = vecs.shape[0]
    lanes = cross.shape[2]
    value_cross = cross_in[0] + cross_in[1] + cross_in[2] + cross_in[3]
    value_vecs = vecs_in[0] + vecs_in[1] + vecs_in[2] + vecs_in[3]
    pieces = [value_cross, own[...]] + [
        value_vecs[:, i * lanes : (i + 1) * lanes] for i in range(vecs.shape[1] // lanes)
    ]
    value = jnp.concatenate(pieces, axis=0)
    for level in range(levels):
        outgo[level] = value
        flow = links.flow()
        sends.append(
            links.start(outgo.at[level], income.at[level], flow, row_peers[level])
        )
        links.arrived(income.at[level], flow, row_peers[level])
        value = outgo[level] + income[level]
    out[...] = value
    for one in sends:
        one.wait_send()


def small_sum(collective_id, row_count, cross, own, vecs):
    levels = doublings(row_count)
    n, kept, lanes = cross.shape
    height = 2 * kept + vecs.shape[0] * vecs.shape[1] // lanes
    flows = 6 + levels
    total = pl.pallas_call(
        functools.partial(small_sum_kernel, levels),
        out_shape=jax.ShapeDtypeStruct((height, lanes), f32),
        in_specs=[pl.BlockSpec(memory_space=VMEM)] * 3,
        out_specs=pl.BlockSpec(memory_space=VMEM),
        scratch_shapes=[
            VMEM((n, kept, lanes), f32),
            VMEM((n,) + vecs.shape, f32),
            VMEM((levels, height, lanes), f32),
            VMEM((levels, height, lanes), f32),
            pltpu.SemaphoreType.DMA((flows,)),
            pltpu.SemaphoreType.DMA((flows,)),
        ],
        compiler_params=pltpu.CompilerParams(
            collective_id=collective_id, has_side_effects=True
        ),
        name="small_sum",
    )(cross, own, vecs)
    parts = total[2 * kept :].reshape(-1, vecs.shape[0], lanes)
    return (
        total[:kept],
        total[kept : 2 * kept],
        jnp.moveaxis(parts, 0, 1).reshape(vecs.shape),
    )


def per_device(
    row_count,
    tokens, memory, out_grad, dec_segments, src_segments,
    self_query, self_key, self_value, self_out,
    cross_query, cross_key, cross_value, cross_out,
    ffn_in, ffn_out, adapt_down, adapt_down_bias, adapt_up, adapt_up_bias,
    self_prefix, cross_prefix, norm_gain, norm_shift,
):
    seq_local, _, width = tokens.shape
    prefix_len = self_prefix.shape[1]
    lanes = self_query.shape[1]
    adapt = adapt_down.shape[1]
    t = lax.axis_index("tp")
    x, mem, grad_in = (a.reshape(seq_local, width) for a in (tokens, memory, out_grad))

    def pack_prefix(prefix):
        return jnp.pad(prefix, ((0, 0), (0, PRE_PACK - prefix_len), (0, 0))).reshape(
            2 * PRE_PACK, lanes
        )

    def unpack_prefix(packed):
        return packed.reshape(2, PRE_PACK, lanes)[:, :prefix_len]

    seq = dec_segments.shape[1]
    never = jnp.full((1, PRE), -1, jnp.int32)
    dec_row = jnp.concatenate([never, dec_segments], axis=1)
    src_row = jnp.concatenate([never, src_segments], axis=1)
    dec_q = dec_segments
    own_q = lax.dynamic_slice(dec_segments, (0, t * seq_local), (1, seq_local))

    gathered = gather_all(
        0,
        x,
        mem,
        pack_prefix(cross_prefix),
        (cross_query, cross_key, cross_value, cross_out, ffn_in, ffn_out),
    )
    x_full, m_full, pre_full = gathered[:3]
    cross_weights = gathered[3:7]
    w_in, w_out = gathered[7:]
    m_full = m_full.reshape(seq, width)

    q1, k1, v1_heads, part = self_forward(
        prefix_len, x_full, self_query, self_key, self_value, self_out,
        pack_prefix(self_prefix), dec_q.reshape(seq, 1), dec_row,
    )
    (resid_one,) = scatter_sum(1, (part,), (x,), (f32,))
    q2, k2, v2_heads, resid_two = cross_forward(
        prefix_len, resid_one, m_full, cross_weights, pre_full,
        own_q.reshape(seq_local, 1), src_row, norm_gain, norm_shift,
    )
    output, dr2, up_part, down_part, vecs_ff = feed_forward(
        resid_two, grad_in, w_in, w_out,
        adapt_down, adapt_down_bias.reshape(1, adapt), adapt_up, adapt_up_bias.reshape(1, width),
        norm_gain, norm_shift,
    )
    adapter = adapter_sum(2, row_count, jnp.concatenate([up_part, down_part], axis=0))
    dr1, dr1_low, dm, cross_pre_part, vecs_cross = cross_backward(
        prefix_len, dr2, resid_one, q2, k2, v2_heads, cross_weights,
        own_q, src_row.reshape(PRE + seq, 1), norm_gain,
    )
    (dr1_full,) = gather_rows(3, dr1_low)
    part, self_pre_part = self_backward(
        prefix_len, dr1_full, q1, k1, v1_heads,
        self_query, self_key, self_value, self_out, dec_q, dec_row.reshape(PRE + seq, 1),
    )
    tokens_grad, memory_grad = scatter_sum(
        4, (part, dm.reshape(part.shape)), (dr1,), (bf16, bf16)
    )
    cross_pre, self_pre, vecs = small_sum(
        5, row_count, cross_pre_part, self_pre_part, vecs_ff + vecs_cross
    )
    local = tokens.shape
    return (
        output.reshape(local),
        tokens_grad.reshape(local),
        memory_grad.reshape(local),
        unpack_prefix(self_pre),
        unpack_prefix(cross_pre),
        vecs[0:3],
        vecs[3:6],
        adapter[adapt:].T.astype(f32),
        vecs[7, :adapt],
        adapter[:adapt].astype(f32),
        vecs[6],
    )


def solution(mesh):
    placed = (
        (P("tp", "rows", None),) * 3
        + (P("rows", None),) * 2
        + (P(None, "tp"),) * 3
        + (P("tp", None),)
        + (P(None, "tp"),) * 3
        + (P("tp", None),)
        + (P(None, "tp"), P("tp", None))
        + (P(),) * 4
        + (P(None, None, "tp"),) * 2
        + (P(),) * 2
    )
    return jax.shard_map(
        functools.partial(per_device, mesh.shape["rows"]),
        mesh=mesh,
        in_specs=placed,
        out_specs=(P("tp", "rows", None),) * 3 + (P(None, None, "tp"),) * 2 + (P(),) * 6,
        check_vma=False,
    )
```

time: 833 us -> 533 us (0.64); the launches traced: 824 us -> 532 us
  waiting for transfers between devices: 516 us -> 0 us
  Pallas kernels: 0 us -> 500 us
  matrix products: 158 us -> 0 us
  other arithmetic: 57.7 us -> 5.08 us
  blocking collectives: 40.4 us -> 0 us
  between operations: 15.4 us -> 1.01 us
  starting transfers between devices: 12 us -> 0 us
    pallas_call x0 -> x11, Pallas kernels: none -> 500 us  [the longest x1 231 us: gather_all(): pl.pallas_call(functools.partial(gather_all_kernel, count), out_shape=tup...]
    psum x2 -> x0, waiting for transfers between devices: 202 us -> none  [the longest x1 130 us: per_device(): lax.psum((jnp.stack([gain_one, gain_two, gain_three]), jnp.stack([shift_o...]
    reduce_scatter x6 -> x0, waiting for transfers between devices: 163 us -> none  [the longest x1 44.4 us: per_device(): lax.psum_scatter(jnp.concatenate([to_query, to_memory], axis=1).astype(jn...]
    dot_general x37 -> x0, matrix products: 158 us -> none  [the longest x25 73.3 us: product(): return jnp.dot(left_side, right_side, preferred_element_type=jnp.float32)]
    all_gather x7 -> x0, waiting for transfers between devices: 149 us -> none  [the longest x1 22.7 us: per_device(): grad_flat = flatten(lax.all_gather(grad_low, 'tp', axis=0, tiled=True))]
    psum x1 -> x0, blocking collectives: 40.4 us -> none  [per_device(): lax.psum((jnp.stack([gain_one, gain_two, gain_three]), jnp.stack([shift_o...]
    reduce_sum x13 -> x0, other arithmetic: 28.3 us -> none  [the longest x2 16.6 us: attend(): row_total = jnp.sum(exponent, axis=2, keepdims=True)]
    convert_element_type x8 -> x2, other arithmetic: 23 us -> 1.93 us  [the longest x1 1.63 us: per_device(): adapter[:adapt].astype(f32)]
  transfers between devices with their start and end apart: 15 -> 0, of which waited for: 14 -> 0; matrix products, arithmetic and copies ran while one was open for 4% -> 0% of each run, Pallas kernels for 0% -> 0%
where the time goes in v1:
time: 533 us; the launch traced here: 532 us
  Pallas kernels  500 us (94%)
  local copies, waits for them, and re-layouts  25.9 us (5%)
    pallas_call x1, Pallas kernels, gather_all(): pl.pallas_call(functools.partial(gather_all_kernel, count), out_shape=tup...  231 us
    pallas_call x1, Pallas kernels, adapter_sum(): pl.pallas_call(functools.partial(adapter_sum_kernel, levels), out_shape=j...  50.9 us
    pallas_call x2, Pallas kernels, scatter_sum(): pl.pallas_call(functools.partial(scatter_kernel, count, len(base)), out_s...  43.5 us
    pallas_call x1, Pallas kernels, cross_backward(): pl.pallas_call(functools.partial(cross_backward_kernel, prefix_len), grid...  38.4 us
    pallas_call x1, Pallas kernels, small_sum(): pl.pallas_call(functools.partial(small_sum_kernel, levels), out_shape=jax...  32.6 us
    pallas_call x1, Pallas kernels, cross_forward(): pl.pallas_call(functools.partial(cross_forward_kernel, prefix_len), grid=...  24 us
    pallas_call x1, Pallas kernels, feed_forward(): pl.pallas_call(feed_forward_kernel, grid=(2 * n,), out_shape=outs, in_spe...  23.6 us
    pallas_call x1, Pallas kernels, self_backward(): pl.pallas_call(functools.partial(self_backward_kernel, prefix_len), out_s...  22 us

profile of v1, /device:TPU:0, one launch (start us, length us, event | category | flops | bytes accessed | tf_op | source)
XLA Modules:
  0.0 532.2 jit_solution(12571939209132968535)
XLA Ops:
  0.6 0.8 copy.54
  1.4 0.6 pad.9.clone
  2.0 0.0 copy-start.8
  2.0 0.0 copy-start.10
  2.1 0.0 copy-start.12
  2.1 231.1 %gather_all.1 = (bf16[4,256,1024]{2,1,0:T(8,128)(2,1)}, bf16[4,256,1024]{2,1,0:T(8,128)(2,1)}, bf16[4,64,256]{2,1,0:T(8,128)(2,1)}, bf16[4,1024,256]{2,1,0:T(8,1...) custom-call(bf16[256,1024]{1,0:T(8,128)(2,1)} %bitcast.43, ...), custom_call_target="tpu_custom_call" | custom-call | tf_op jit(solution)/shard_map/gather_all/pallas_call | solution.py:708
  233.2 0.0 copy-done.27
  233.2 0.0 copy-done.30
  233.2 0.2 copy.43.seg_col
  233.5 0.0 copy-done.29
  233.5 0.0 copy-done.6
  233.5 0.0 copy-done.8
  233.5 0.0 copy-done.10
  233.5 0.0 copy-done.12
  233.5 0.0 copy-start.1
  233.5 15.2 %self_forward.1 = (bf16[1024,256]{1,0:T(8,128)(2,1)S(1)}, bf16[1152,256]{1,0:T(8,128)(2,1)S(1)}, bf16[1152,256]{1,0:T(8,128)(2,1)S(1)}, bf16[4,256,1024]{2,1,0:T(8,128)(2,1)}) custom-call(bf16[1024,1024]{1,0:T(8,128)(2,1)} %bitcast.52, bf16[1024,256]{1,0:T(8,128)(2,1)S(1)} %copy-done.6, bf16[1024,256]{1,0:T(8,128)(2,1)S(1)} %copy-done.8, ...), custom_call_target="tpu_custom_call" | custom-call | tf_op jit(solution)/shard_map/self_forward/pallas_call | solution.py:149
  248.8 0.0 copy-done.1
  248.8 0.0 copy-start.2
  248.8 2.2 copy-done.2
  251.0 16.3 %scatter_sum.2.v1 = f32[256,1024]{1,0:T(8,128)S(1)} custom-call(bf16[4,256,1024]{2,1,0:T(8,128)(2,1)S(1)} %copy-done.2, bf16[256,1024]{1,0:T(8,128)(2,1)S(1)} %bitcast.44), custom_call_target="tpu_custom_call" | custom-call | tf_op jit(solution)/shard_map/scatter_sum/pallas_call | solution.py:777
  267.3 0.0 copy-done.16
  267.3 0.0 copy-start
  267.3 0.0 copy-done.18
  267.3 0.0 copy-done.21
  267.3 0.1 copy.44.seg_col
  267.5 24.0 %cross_forward.1 = (bf16[4,256,256]{2,1,0:T(8,128)(2,1)S(1)}, bf16[4,1152,256]{2,1,0:T(8,128)(2,1)}, bf16[4,1152,256]{2,1,0:T(8,128)(2,1)}, f32[256,1024]{1,0:T(8,128)S(1)}) custom-call(f32[256,1024]{1,0:T(8,128)S(1)} %scatter_sum.2.v1, bf16[1024,1024]{1,0:T(8,128)(2,1)S(1)} %bitcast.46, bf16[4,1024,256]{2,1,0:T(8,128)(2,1)} %get-tuple-element.45.wq, ...), custom_call_target="tpu_custom_call" | custom-call | tf_op jit(solution)/shard_map/cross_forward/pallas_call | solution.py:231
  291.5 1.0 copy-done.15
  292.5 0.8 copy-done.20
  293.3 23.6 %feed_forward.1 = (bf16[256,1024]{1,0:T(8,128)(2,1)}, f32[256,1024]{1,0:T(8,128)}, bf16[512,1024]{1,0:T(8,128)(2,1)}, bf16[512,1024]{1,0:T(8,128)(2,1)}, f32[8,1024]{1,0:T(8,128)}) custom-call(f32[256,1024]{1,0:T(8,128)} %copy-done.15, bf16[256,1024]{1,0:T(8,128)(2,1)} %bitcast.54, bf16[4,1024,1024]{2,1,0:T(8,128)(2,1)} %get-tuple-element.51.w_in, ...), custom_call_target="tpu_custom_call" | custom-call | tf_op jit(solution)/shard_map/feed_forward/pallas_call | solution.py:319
  316.9 1.7 pad_maximum_fusion
  318.6 50.9 %adapter_sum.1 = bf16[2,2,4,64,1024]{4,3,2,1,0:T(8,128)(2,1)S(1)} custom-call(bf16[2,2,4,64,1024]{4,3,2,1,0:T(8,128)(2,1)S(1)} %bitcast.42), custom_call_target="tpu_custom_call" | custom-call | tf_op jit(solution)/shard_map/adapter_sum/pallas_call | solution.py:872
  369.5 0.2 fusion
  369.7 0.3 bitcast_convert_fusion.1
  370.0 1.8 copy.51
  371.8 1.6 bitcast_convert_fusion
  373.5 0.6 constant_dynamic-slice_fusion.seg_row
  374.0 1.1 copy.45.seg_col
  375.1 38.4 %cross_backward.1 = (f32[256,1024]{1,0:T(8,128)}, bf16[256,1024]{1,0:T(8,128)(2,1)}, bf16[1024,1024]{1,0:T(8,128)(2,1)}, f32[4,64,256]{2,1,0:T(8,128)}, f32[8,1024]{1,0:T(8,128)}) custom-call(f32[256,1024]{1,0:T(8,128)} %get-tuple-element.54.dr2, f32[256,1024]{1,0:T(8,128)} %copy-done, bf16[4,256,256]{2,1,0:T(8,128)(2,1)} %copy-done.20, ...), custom_call_target="tpu_custom_call" | custom-call | tf_op jit(solution)/shard_map/cross_backward/pallas_call | solution.py:417
  413.5 0.0 copy-start.7
  413.5 1.4 add.15.vecs
  415.0 18.9 %gather_rows.1.dr1 = bf16[4,256,1024]{2,1,0:T(8,128)(2,1)} custom-call(bf16[256,1024]{1,0:T(8,128)(2,1)} %get-tuple-element.58.refs_0_), custom_call_target="tpu_custom_call" | custom-call | tf_op jit(solution)/shard_map/gather_rows/pallas_call | solution.py:609
  433.9 0.2 copy.46.seg_col
  434.1 0.0 copy-start.9
  434.1 1.0 copy-done.9
  435.2 1.0 copy-done.11
  436.2 1.0 copy-done.13
  437.3 1.1 copy-done.17
  438.3 1.1 copy-done.19
  439.4 1.0 copy-done.22
  440.4 22.0 %self_backward.1 = (bf16[4,256,1024]{2,1,0:T(8,128)(2,1)}, f32[64,256]{1,0:T(8,128)S(1)}) custom-call(bf16[4,256,1024]{2,1,0:T(8,128)(2,1)} %gather_rows.1.dr1, bf16[1024,256]{1,0:T(8,128)(2,1)S(1)} %copy-done.22, bf16[1152,256]{1,0:T(8,128)(2,1)S(1)} %copy-done.17, bf16[1152,256]{1,0:T(8,128)(2,1)S(1)} %copy-done.19, bf16[1024,256]{1,0:T(8,128)(2,1)S(1)} %copy-done.7, ...), custom_call_target="tpu_custom_call" | custom-call | tf_op jit(solution)/shard_map/self_backward/pallas_call | solution.py:487
  462.4 0.6 copy-done.25
  463.0 32.6 %small_sum.1 = f32[160,256]{1,0:T(8,128)} custom-call(f32[4,64,256]{2,1,0:T(8,128)} %get-tuple-element.67.cross, f32[64,256]{1,0:T(8,128)} %copy-done.25, f32[8,1024]{1,0:T(8,128)} %add.15.vecs), custom_call_target="tpu_custom_call" | custom-call | tf_op jit(solution)/shard_map/small_sum/pallas_call | solution.py:941
  495.7 0.9 fusion.2
  496.6 0.7 copy.52
  497.2 0.7 copy.53
  497.9 0.8 fusion.1
  498.7 0.6 fusion.3
  499.3 0.6 slice.60
  499.9 0.6 slice.59
  500.5 1.6 copy-done.4
  502.1 1.2 copy-done.14
  503.3 27.3 %scatter_sum.3 = (bf16[256,1024]{1,0:T(8,128)(2,1)S(1)}, bf16[256,1024]{1,0:T(8,128)(2,1)S(1)}) custom-call(bf16[4,256,1024]{2,1,0:T(8,128)(2,1)S(1)} %copy-done.4, bf16[4,256,1024]{2,1,0:T(8,128)(2,1)S(1)} %bitcast.45, f32[256,1024]{1,0:T(8,128)S(1)} %copy-done.14), custom_call_target="tpu_custom_call" | custom-call | tf_op jit(solution)/shard_map/scatter_sum/pallas_call | solution.py:777
  530.6 0.8 copy.58
  531.4 0.8 copy.59
  (35 shorter events, 0.1 us)
Async XLA Ops:
  2.0 231.2 %copy-start.27 = (s32[1,1024]{1,0:T(1,128)S(1)}, s32[1,1024]{1,0:T(1,128)}, u32[]{:S(2)}) copy-start(s32[1,1024]{1,0:T(1,128)} %seg_row.1) | copy-start | bytes 12292
  2.0 231.2 %copy-start.30 = (s32[1,1024]{1,0:T(1,128)S(1)}, s32[1,1024]{1,0:T(1,128)}, u32[]{:S(2)}) copy-start(s32[1,1024]{1,0:T(1,128)} %param.27) | copy-start | bytes 12292
  2.0 231.4 %copy-start.29 = (bf16[2,30,256]{2,0,1:T(2,128)(2,1)S(1)}, bf16[2,30,256]{2,0,1:T(2,128)(2,1)}, u32[]{:S(2)}) copy-start(bf16[2,30,256]{2,0,1:T(2,128)(2,1)} %param.42) | copy-start | bytes 92164
  2.0 231.5 %copy-start.6 = (bf16[1024,256]{1,0:T(8,128)(2,1)S(1)}, bf16[1024,256]{1,0:T(8,128)(2,1)}, u32[]{:S(2)}) copy-start(bf16[1024,256]{1,0:T(8,128)(2,1)} %wq.3) | copy-start | bytes 1572868
  2.0 231.5 %copy-start.8 = (bf16[1024,256]{1,0:T(8,128)(2,1)S(1)}, bf16[1024,256]{1,0:T(8,128)(2,1)}, u32[]{:S(2)}) copy-start(bf16[1024,256]{1,0:T(8,128)(2,1)} %wk.3) | copy-start | bytes 1572868
  2.0 231.5 %copy-start.10 = (bf16[1024,256]{1,0:T(8,128)(2,1)S(1)}, bf16[1024,256]{1,0:T(8,128)(2,1)}, u32[]{:S(2)}) copy-start(bf16[1024,256]{1,0:T(8,128)(2,1)} %wv.3) | copy-start | bytes 1572868
  2.1 231.5 %copy-start.12 = (bf16[256,1024]{1,0:T(8,128)(2,1)S(1)}, bf16[256,1024]{1,0:T(8,128)(2,1)}, u32[]{:S(2)}) copy-start(bf16[256,1024]{1,0:T(8,128)(2,1)} %wo.3) | copy-start | bytes 1572868
  233.5 15.2 %copy-start.1 = (bf16[256,1,1024]{2,0,1:T(8,128)(2,1)S(1)}, bf16[256,1,1024]{2,0,1:T(8,128)(2,1)}, u32[]{:S(2)}) copy-start(bf16[256,1,1024]{2,0,1:T(8,128)(2,1)} %param.23) | copy-start | bytes 1572868
  248.8 18.5 %copy-start.16 = (bf16[1152,256]{1,0:T(8,128)(2,1)}, bf16[1152,256]{1,0:T(8,128)(2,1)S(1)}, u32[]{:S(2)}) copy-start(bf16[1152,256]{1,0:T(8,128)(2,1)S(1)} %get-tuple-element.60.k) | copy-start | bytes 1769476
  248.8 18.5 %copy-start.18 = (bf16[1152,256]{1,0:T(8,128)(2,1)}, bf16[1152,256]{1,0:T(8,128)(2,1)S(1)}, u32[]{:S(2)}) copy-start(bf16[1152,256]{1,0:T(8,128)(2,1)S(1)} %get-tuple-element.61.v) | copy-start | bytes 1769476
  248.8 18.5 %copy-start.21 = (bf16[1024,256]{1,0:T(8,128)(2,1)}, bf16[1024,256]{1,0:T(8,128)(2,1)S(1)}, u32[]{:S(2)}) copy-start(bf16[1024,256]{1,0:T(8,128)(2,1)S(1)} %get-tuple-element.59.q) | copy-start | bytes 1572868
  248.8 2.2 copy-start.2
  251.0 16.5 %copy-start.5 = (bf16[4,256,1024]{2,1,0:T(8,128)(2,1)S(1)}, bf16[4,256,1024]{2,1,0:T(8,128)(2,1)}, u32[]{:S(2)}) copy-start(bf16[4,256,1024]{2,1,0:T(8,128)(2,1)} %get-tuple-element.44) | copy-start | bytes 6291460
  251.0 16.5 %copy-start.23 = (f32[3,1024]{1,0:T(4,128)S(1)}, f32[3,1024]{1,0:T(4,128)}, u32[]{:S(2)}) copy-start(f32[3,1024]{1,0:T(4,128)} %gain.5) | copy-start | bytes 36868
  251.0 16.5 %copy-start.24 = (bf16[4,64,256]{2,1,0:T(8,128)(2,1)S(1)}, bf16[4,64,256]{2,1,0:T(8,128)(2,1)}, u32[]{:S(2)}) copy-start(bf16[4,64,256]{2,1,0:T(8,128)(2,1)} %get-tuple-element.49.pre) | copy-start | bytes 393220
  251.0 16.5 %copy-start.26 = (f32[3,1024]{1,0:T(4,128)S(1)}, f32[3,1024]{1,0:T(4,128)}, u32[]{:S(2)}) copy-start(f32[3,1024]{1,0:T(4,128)} %shift.3) | copy-start | bytes 36868
  267.3 24.2 %copy-start = (f32[256,1024]{1,0:T(8,128)}, f32[256,1024]{1,0:T(8,128)S(1)}, u32[]{:S(2)}) copy-start(f32[256,1024]{1,0:T(8,128)S(1)} %scatter_sum.2.v1) | copy-start | bytes 3145732
  291.5 1.0 copy-start.15
  292.5 0.8 copy-start.20
  375.1 38.4 %copy-start.28 = (f32[8,1024]{1,0:T(8,128)S(1)}, f32[8,1024]{1,0:T(8,128)}, u32[]{:S(2)}) copy-start(f32[8,1024]{1,0:T(8,128)} %get-tuple-element.69) | copy-start | bytes 98308
  413.5 20.6 %copy-start.7 = (bf16[1024,256]{1,0:T(8,128)(2,1)S(1)}, bf16[1024,256]{1,0:T(8,128)(2,1)}, u32[]{:S(2)}) copy-start(bf16[1024,256]{1,0:T(8,128)(2,1)} %wq.3) | copy-start | bytes 1572868
  434.1 1.0 copy-start.9
  435.2 1.0 copy-start.11
  436.2 1.0 copy-start.13
  437.3 1.1 copy-start.17
  438.3 1.1 copy-start.19
  439.4 1.0 copy-start.22
  440.4 60.0 %copy-start.3 = (bf16[1024,1024]{1,0:T(8,128)(2,1)S(1)}, bf16[1024,1024]{1,0:T(8,128)(2,1)}, u32[]{:S(2)}) copy-start(bf16[1024,1024]{1,0:T(8,128)(2,1)} %get-tuple-element.63) | copy-start | bytes 6291460
  462.4 0.6 copy-start.25
  500.5 1.6 copy-start.4
  502.1 1.2 copy-start.14
